TPU v7x, 128 devices: a whole 4x4x4 slice. The times are simulated.
128 devices in a mesh: lon: 32 (over z, x, core), lat: 4 (over y).
Axes of the slice: x: 4, y: 4, z: 4, core: 2. Of those that a mesh axis runs over, the one named last changes fastest.
Arguments:
- guide: float32 [512, 32768], P('lat', 'lon'), may hold values from -8 to 8
- screen: float32 [512, 32768], P('lat', 'lon'), may hold values from 0.001 to 0.1
- valid: int32 [512, 32768], P('lat', 'lon'), may hold values 0 or 1
- tiles: int32 [4, 256], P('lat', 'lon'), may hold values 0 or 1
Outputs:
- solution_field: float32 [512, 32768], P('lat', 'lon')
- residual: float32 [512, 32768], P('lat', 'lon')
All inputs are finite; a program needn't handle non-finite values. No bound on the sum of `valid` or of `tiles` on one device may be relied on, other than what follows from the above.
Results may differ from a plain program's by a relative error of at most 0.00012.
Values sent between devices are 32-bit elements; how exact they have to be, the bound alone decides.
A program may use at most 128 MiB of HBM per device.

v0:
```python
import jax
import jax.numpy as jnp
from jax import lax
from jax.sharding import PartitionSpec as P

TILE = 128
LEVELS = 4
SMOOTH = 2
COARSE_SWEEPS = 8
CYCLES = 2


OMEGA = 0.8


def padded(block, sides, width, periodic):
    for axis, dim in sides:
        count = lax.axis_size(axis)
        forward = [(i, i + 1) for i in range(count - 1)]
        if periodic:
            forward.append((count - 1, 0))
        backward = [(target, source) for source, target in forward]
        low = lax.ppermute(
            lax.slice_in_dim(block, block.shape[dim] - width, None, axis=dim), axis, forward
        )
        high = lax.ppermute(lax.slice_in_dim(block, 0, width, axis=dim), axis, backward)
        block = jnp.concatenate([low, block, high], axis=dim)
    return block


def local_stencil(field, weight):
    rowed = padded(field, (("lat", 0),), 1, False)
    coled = padded(field, (("lon", 1),), 1, True)
    upper = rowed[:-2]
    lower = rowed[2:]
    left = coled[:, :-2]
    right = coled[:, 2:]
    return (4.0 + weight) * field - (upper + lower + left + right)


def relax_with(apply_op, field, source, weight, active):
    return field + OMEGA * active * (source - apply_op(field, weight)) / (4.0 + weight)


def block_sum(field):
    rows, cols = field.shape
    return field.reshape(rows // 2, 2, cols // 2, 2).sum(axis=(1, 3))


def block_max(field):
    rows, cols = field.shape
    return field.reshape(rows // 2, 2, cols // 2, 2).max(axis=(1, 3))


def expand(field):
    return jnp.repeat(jnp.repeat(field, 2, 0), 2, 1)


def body(guide, screen, valid, tiles):
    flags = jnp.repeat(jnp.repeat(tiles.astype(jnp.float32), TILE, 0), TILE, 1)
    active = valid.astype(jnp.float32) * flags
    weights = [screen]
    actives = [active]
    for level in range(LEVELS - 1):
        weights.append(block_sum(weights[-1]))
        actives.append(block_max(actives[-1]))

    def coarsest(level_src):
        field = jnp.zeros_like(level_src)
        for sweep in range(COARSE_SWEEPS):
            field = relax_with(local_stencil, field, level_src, weights[-1], actives[-1])
        return field

    source = active * guide
    solution_field = jnp.zeros_like(guide)

    def vcycle(level, level_src):
        if level == LEVELS - 1:
            return coarsest(level_src)
        field = jnp.zeros_like(level_src)
        for sweep in range(SMOOTH):
            field = relax_with(local_stencil, field, level_src, weights[level], actives[level])
        resid = actives[level] * (level_src - local_stencil(field, weights[level]))
        coarse_src = actives[level + 1] * block_sum(resid)
        correction = vcycle(level + 1, coarse_src)
        field = field + actives[level] * expand(correction)
        for sweep in range(SMOOTH):
            field = relax_with(local_stencil, field, level_src, weights[level], actives[level])
        return field

    for cycle in range(CYCLES):
        resid = active * (source - local_stencil(solution_field, screen))
        solution_field = solution_field + vcycle(0, resid)
    residual = active * (source - local_stencil(solution_field, screen))
    return (solution_field, residual)


def solution(mesh):
    return jax.shard_map(
        body,
        mesh=mesh,
        in_specs=(P("lat", "lon"), P("lat", "lon"), P("lat", "lon"), P("lat", "lon")),
        out_specs=(P("lat", "lon"), P("lat", "lon")),
        check_vma=False,
    )
```

profile of v0, /device:TPU:0, one launch (start us, length us, event | category | flops | bytes accessed | tf_op | source)
XLA Modules:
  0.0 884.3 jit_solution(1468419304482706146)
XLA Ops:
  5.8 5.5 collective-permute-start.3
  52.1 34.9 %reshape.82 = f32[64,2,512,2]{3,2,1,0:T(8,128)} reshape(f32[128,1024]{1,0:T(8,128)S(1)} %copy-done.1) | data formatting | bytes 1048576 | tf_op jit(solution)/shard_map/reshape | solution.py:47
  87.0 13.2 %reduce_sum.82 = f32[64,512]{1,0:T(8,128)S(1)} reduce(f32[64,2,512,2]{3,2,1,0:T(8,128)} %reshape.82, f32[]{:T(128)} %constant.6.clone.1), dimensions={1,3}, to_apply=%region_2.0 | reduce | flops 98304 | bytes 655364 | tf_op jit(solution)/shard_map/reduce_sum | solution.py:47
  100.5 34.9 %reshape.80 = f32[64,2,512,2]{3,2,1,0:T(8,128)} reshape(f32[128,1024]{1,0:T(8,128)S(1)} %copy.51) | data formatting | bytes 1048576 | tf_op jit(solution)/shard_map/reshape | solution.py:52
  135.3 13.2 %reduce_max.27 = f32[64,512]{1,0:T(8,128)S(1)} reduce(f32[64,2,512,2]{3,2,1,0:T(8,128)} %reshape.80, f32[]{:T(128)} %constant.7.clone.1), dimensions={1,3}, to_apply=%region_0.0 | reduce | flops 98304 | bytes 655364 | tf_op jit(solution)/shard_map/reduce_max | solution.py:52
  148.6 5.1 collective-permute-start.15
  164.4 34.9 %reshape.81 = f32[64,2,512,2]{3,2,1,0:T(8,128)} reshape(f32[128,1024]{1,0:T(8,128)S(1)} %copy.52) | data formatting | bytes 1048576 | tf_op jit(solution)/shard_map/reshape | solution.py:47
  199.2 13.2 %reduce_sum.81 = f32[64,512]{1,0:T(8,128)S(1)} reduce(f32[64,2,512,2]{3,2,1,0:T(8,128)} %reshape.81, f32[]{:T(128)} %constant.6.clone.1), dimensions={1,3}, to_apply=%region_1.0 | reduce | flops 98304 | bytes 655364 | tf_op jit(solution)/shard_map/reduce_sum | solution.py:47
  218.6 5.1 collective-permute-start.19
  223.7 9.7 %reshape.85 = f32[32,2,256,2]{3,2,1,0:T(8,128)} reshape(f32[64,512]{1,0:T(8,128)S(1)} %reduce_sum.82) | data formatting | bytes 262144 | tf_op jit(solution)/shard_map/reshape | solution.py:47
  254.5 9.7 %reshape.83 = f32[32,2,256,2]{3,2,1,0:T(8,128)} reshape(f32[64,512]{1,0:T(8,128)S(1)} %reduce_max.27) | data formatting | bytes 262144 | tf_op jit(solution)/shard_map/reshape | solution.py:52
  278.7 9.7 %reshape.84 = f32[32,2,256,2]{3,2,1,0:T(8,128)} reshape(f32[64,512]{1,0:T(8,128)S(1)} %fusion.130) | data formatting | bytes 262144 | tf_op jit(solution)/shard_map/reshape | solution.py:47
  336.6 5.1 collective-permute-start.43
  349.1 5.1 collective-permute-start.47
  399.2 5.1 collective-permute-start.63
  411.7 5.1 collective-permute-start.67
  424.4 5.1 collective-permute-start.71
  453.1 5.1 collective-permute-start.79
  481.3 5.1 collective-permute-start.87
  509.0 6.1 collective-permute-start.95
  523.3 8.5 collective-permute-start.99
  539.5 9.6 %collective-permute-start.103 = (f32[128,1]{0,1:T(1,128)S(1)}, f32[128,1]{0,1:T(1,128)S(1)}, u32[]{:S(2)}, u32[]{:S(2)}) collective-permute-start(f32[128,1]{0,1:T(1,128)S(1)} %get-tuple-element.42), channel_id=1, source_target_pairs={{4,0},{8,4},{12,8},{16,12},{20,16},{24,20},{28,24},{32,28},{36,32}... | collective-permute-start | bytes 1544 | tf_op jit(solution)/shard_map/ppermute | solution.py:26
  553.7 35.6 %reshape.95 = f32[64,2,512,2]{3,2,1,0:T(8,128)} reshape(f32[128,1024]{1,0:T(8,128)} %copy.58) | data formatting | bytes 1048576 | tf_op jit(solution)/shard_map/reshape | solution.py:47
  589.3 13.9 %reduce_sum.87 = f32[64,512]{1,0:T(8,128)} reduce(f32[64,2,512,2]{3,2,1,0:T(8,128)} %reshape.95, f32[]{:T(128)} %constant.6.clone.1), dimensions={1,3}, to_apply=%region_9.0 | reduce | flops 98304 | bytes 655364 | tf_op jit(solution)/shard_map/reduce_sum | solution.py:47
  609.9 10.5 %collective-permute-start.107 = (f32[64,1]{1,0:T(8,128)S(1)}, f32[64,1]{1,0:T(8,128)S(1)}, u32[]{:S(2)}, u32[]{:S(2)}) collective-permute-start(f32[64,1]{1,0:T(8,128)S(1)} %get-tuple-element.82), channel_id=1, source_target_pairs={{4,0},{8,4},{12,8},{16,12},{20,16},{24,20},{28,24},{32,28},{36,32}... | collective-permute-start | bytes 776 | tf_op jit(solution)/shard_map/ppermute | solution.py:26
  627.9 5.1 collective-permute-start.111
  635.4 10.4 %reshape.96 = f32[32,2,256,2]{3,2,1,0:T(8,128)} reshape(f32[64,512]{1,0:T(8,128)} %fusion.100) | data formatting | bytes 262144 | tf_op jit(solution)/shard_map/reshape | solution.py:47
  657.1 5.1 collective-permute-start.115
  669.7 5.2 collective-permute-start.119
  703.1 5.1 collective-permute-start.127
  826.6 5.3 collective-permute-start.163
  871.7 6.1 collective-permute-start.175
  (549 shorter events, 530.5 us)
Async XLA Ops:
  0.7 15.9 %collective-permute-start = (f32[1,1024]{0,1:T(8,128)S(1)}, f32[1,1024]{0,1:T(8,128)S(1)}, u32[]{:S(2)}, u32[]{:S(2)}) collective-permute-start(f32[1,1024]{0,1:T(8,128)S(1)} %broadcast.100), channel_id=1, source_target_pairs={{0,1},{1,2},{2,3},{4,5},{5,6},{6,7},{8,9},{9,10},{10,11},{12,13},{... | collective-permute-start | bytes 12296 | tf_op jit(solution)/shard_map/ppermute | solution.py:23
  4.4 15.4 %collective-permute-start.1 = (f32[1,1024]{0,1:T(8,128)S(1)}, f32[1,1024]{0,1:T(8,128)}, u32[]{:S(2)}, u32[]{:S(2)}) collective-permute-start(f32[1,1024]{0,1:T(8,128)S(1)} %broadcast.100), channel_id=1, source_target_pairs={{1,0},{2,1},{3,2},{5,4},{6,5},{7,6},{9,8},{10,9},{11,10},{13,12},{... | collective-permute-start | bytes 12296 | tf_op jit(solution)/shard_map/ppermute | solution.py:26
  22.5 13.4 %collective-permute-start.4 = (f32[1,1024]{0,1:T(8,128)S(1)}, f32[1,1024]{0,1:T(8,128)S(1)}, u32[]{:S(2)}, u32[]{:S(2)}) collective-permute-start(f32[1,1024]{0,1:T(8,128)S(1)} %get-tuple-element.63), channel_id=1, source_target_pairs={{0,1},{1,2},{2,3},{4,5},{5,6},{6,7},{8,9},{9,10},{10,11},{12,13},{... | collective-permute-start | bytes 12296 | tf_op jit(solution)/shard_map/ppermute | solution.py:23
  26.0 14.1 %collective-permute-start.5 = (f32[1,1024]{0,1:T(8,128)S(1)}, f32[1,1024]{0,1:T(8,128)S(1)}, u32[]{:S(2)}, u32[]{:S(2)}) collective-permute-start(f32[1,1024]{0,1:T(8,128)S(1)} %get-tuple-element.64), channel_id=1, source_target_pairs={{1,0},{2,1},{3,2},{5,4},{6,5},{7,6},{9,8},{10,9},{11,10},{13,12},{... | collective-permute-start | bytes 12296 | tf_op jit(solution)/shard_map/ppermute | solution.py:26
  41.7 116.5 %collective-permute-start.8 = (f32[1,1024]{0,1:T(8,128)}, f32[1,1024]{0,1:T(8,128)}, u32[]{:S(2)}, u32[]{:S(2)}) collective-permute-start(f32[1,1024]{0,1:T(8,128)} %get-tuple-element.59), channel_id=1, source_target_pairs={{0,1},{1,2},{2,3},{4,5},{5,6},{6,7},{8,9},{9,10},{10,11},{12,13},{... | collective-permute-start | bytes 12296 | tf_op jit(solution)/shard_map/ppermute | solution.py:23
  45.7 113.9 %collective-permute-start.9 = (f32[1,1024]{0,1:T(8,128)}, f32[1,1024]{0,1:T(8,128)}, u32[]{:S(2)}, u32[]{:S(2)}) collective-permute-start(f32[1,1024]{0,1:T(8,128)} %get-tuple-element.60), channel_id=1, source_target_pairs={{1,0},{2,1},{3,2},{5,4},{6,5},{7,6},{9,8},{10,9},{11,10},{13,12},{... | collective-permute-start | bytes 12296 | tf_op jit(solution)/shard_map/ppermute | solution.py:26
  47.0 101.6 %collective-permute-start.10 = (f32[128,1]{0,1:T(1,128)S(1)}, f32[128,1]{0,1:T(1,128)S(1)}, u32[]{:S(2)}, u32[]{:S(2)}) collective-permute-start(f32[128,1]{0,1:T(1,128)S(1)} %get-tuple-element.61), channel_id=1, source_target_pairs={{0,4},{4,8},{8,12},{12,16},{16,20},{20,24},{24,28},{28,32},{32,36}... | collective-permute-start | bytes 1544 | tf_op jit(solution)/shard_map/ppermute | solution.py:23
  47.1 106.6 %collective-permute-start.11 = (f32[128,1]{0,1:T(1,128)S(1)}, f32[128,1]{0,1:T(1,128)S(1)}, u32[]{:S(2)}, u32[]{:S(2)}) collective-permute-start(f32[128,1]{0,1:T(1,128)S(1)} %get-tuple-element.62), channel_id=1, source_target_pairs={{4,0},{8,4},{12,8},{16,12},{20,16},{24,20},{28,24},{32,28},{36,32}... | collective-permute-start | bytes 1544 | tf_op jit(solution)/shard_map/ppermute | solution.py:26
  52.1 160.4 %collective-permute-start.14 = (f32[64,1]{1,0:T(8,128)S(1)}, f32[64,1]{1,0:T(8,128)S(1)}, u32[]{:S(2)}, u32[]{:S(2)}) collective-permute-start(f32[64,1]{1,0:T(8,128)S(1)} %broadcast.106), channel_id=1, source_target_pairs={{0,4},{4,8},{8,12},{12,16},{16,20},{20,24},{24,28},{28,32},{32,36}... | collective-permute-start | bytes 776 | tf_op jit(solution)/shard_map/ppermute | solution.py:23
  148.6 63.9 %collective-permute-start.15 = (f32[64,1]{1,0:T(8,128)S(1)}, f32[64,1]{1,0:T(8,128)S(1)}, u32[]{:S(2)}, u32[]{:S(2)}) collective-permute-start(f32[64,1]{1,0:T(8,128)S(1)} %broadcast.106), channel_id=1, source_target_pairs={{4,0},{8,4},{12,8},{16,12},{20,16},{24,20},{28,24},{32,28},{36,32}... | collective-permute-start | bytes 776 | tf_op jit(solution)/shard_map/ppermute | solution.py:26
  153.7 58.8 %collective-permute-start.12 = (f32[1,512]{1,0:T(1,128)S(1)}, f32[1,512]{1,0:T(1,128)S(1)}, u32[]{:S(2)}, u32[]{:S(2)}) collective-permute-start(f32[1,512]{1,0:T(1,128)S(1)} %broadcast.105), channel_id=1, source_target_pairs={{0,1},{1,2},{2,3},{4,5},{5,6},{6,7},{8,9},{9,10},{10,11},{12,13},{... | collective-permute-start | bytes 6152 | tf_op jit(solution)/shard_map/ppermute | solution.py:23
  158.3 54.3 %collective-permute-start.13 = (f32[1,512]{1,0:T(1,128)S(1)}, f32[1,512]{1,0:T(1,128)S(1)}, u32[]{:S(2)}, u32[]{:S(2)}) collective-permute-start(f32[1,512]{1,0:T(1,128)S(1)} %broadcast.105), channel_id=1, source_target_pairs={{1,0},{2,1},{3,2},{5,4},{6,5},{7,6},{9,8},{10,9},{11,10},{13,12},{... | collective-permute-start | bytes 6152 | tf_op jit(solution)/shard_map/ppermute | solution.py:26
  160.2 132.8 %collective-permute-start.26 = (f32[32,1]{1,0:T(8,128)}, f32[32,1]{1,0:T(8,128)}, u32[]{:S(2)}, u32[]{:S(2)}) collective-permute-start(f32[32,1]{1,0:T(8,128)} %broadcast.111), channel_id=1, source_target_pairs={{0,4},{4,8},{8,12},{12,16},{16,20},{20,24},{24,28},{28,32},{32,36}... | collective-permute-start | bytes 392 | tf_op jit(solution)/shard_map/ppermute | solution.py:23
  212.7 30.6 %collective-permute-start.16 = (f32[1,512]{1,0:T(1,128)S(1)}, f32[1,512]{1,0:T(1,128)S(1)}, u32[]{:S(2)}, u32[]{:S(2)}) collective-permute-start(f32[1,512]{1,0:T(1,128)S(1)} %get-tuple-element.95), channel_id=1, source_target_pairs={{0,1},{1,2},{2,3},{4,5},{5,6},{6,7},{8,9},{9,10},{10,11},{12,13},{... | collective-permute-start | bytes 6152 | tf_op jit(solution)/shard_map/ppermute | solution.py:23
  217.2 26.1 %collective-permute-start.17 = (f32[1,512]{1,0:T(1,128)S(1)}, f32[1,512]{1,0:T(1,128)S(1)}, u32[]{:S(2)}, u32[]{:S(2)}) collective-permute-start(f32[1,512]{1,0:T(1,128)S(1)} %get-tuple-element.96), channel_id=1, source_target_pairs={{1,0},{2,1},{3,2},{5,4},{6,5},{7,6},{9,8},{10,9},{11,10},{13,12},{... | collective-permute-start | bytes 6152 | tf_op jit(solution)/shard_map/ppermute | solution.py:26
  218.6 24.7 %collective-permute-start.18 = (f32[64,1]{1,0:T(8,128)S(1)}, f32[64,1]{1,0:T(8,128)S(1)}, u32[]{:S(2)}, u32[]{:S(2)}) collective-permute-start(f32[64,1]{1,0:T(8,128)S(1)} %get-tuple-element.97), channel_id=1, source_target_pairs={{0,4},{4,8},{8,12},{12,16},{16,20},{20,24},{24,28},{28,32},{32,36}... | collective-permute-start | bytes 776 | tf_op jit(solution)/shard_map/ppermute | solution.py:23
  218.6 24.7 %collective-permute-start.19 = (f32[64,1]{1,0:T(8,128)S(1)}, f32[64,1]{1,0:T(8,128)S(1)}, u32[]{:S(2)}, u32[]{:S(2)}) collective-permute-start(f32[64,1]{1,0:T(8,128)S(1)} %get-tuple-element.98), channel_id=1, source_target_pairs={{4,0},{8,4},{12,8},{16,12},{20,16},{24,20},{28,24},{32,28},{36,32}... | collective-permute-start | bytes 776 | tf_op jit(solution)/shard_map/ppermute | solution.py:26
  243.5 33.5 %collective-permute-start.20 = (f32[1,512]{1,0:T(1,128)S(1)}, f32[1,512]{1,0:T(1,128)S(1)}, u32[]{:S(2)}, u32[]{:S(2)}) collective-permute-start(f32[1,512]{1,0:T(1,128)S(1)} %get-tuple-element.91), channel_id=1, source_target_pairs={{0,1},{1,2},{2,3},{4,5},{5,6},{6,7},{8,9},{9,10},{10,11},{12,13},{... | collective-permute-start | bytes 6152 | tf_op jit(solution)/shard_map/ppermute | solution.py:23
  248.0 30.2 %collective-permute-start.21 = (f32[1,512]{1,0:T(1,128)S(1)}, f32[1,512]{1,0:T(1,128)S(1)}, u32[]{:S(2)}, u32[]{:S(2)}) collective-permute-start(f32[1,512]{1,0:T(1,128)S(1)} %get-tuple-element.92), channel_id=1, source_target_pairs={{1,0},{2,1},{3,2},{5,4},{6,5},{7,6},{9,8},{10,9},{11,10},{13,12},{... | collective-permute-start | bytes 6152 | tf_op jit(solution)/shard_map/ppermute | solution.py:26
  249.4 22.8 %collective-permute-start.22 = (f32[64,1]{1,0:T(8,128)S(1)}, f32[64,1]{1,0:T(8,128)S(1)}, u32[]{:S(2)}, u32[]{:S(2)}) collective-permute-start(f32[64,1]{1,0:T(8,128)S(1)} %get-tuple-element.93), channel_id=1, source_target_pairs={{0,4},{4,8},{8,12},{12,16},{16,20},{20,24},{24,28},{28,32},{32,36}... | collective-permute-start | bytes 776 | tf_op jit(solution)/shard_map/ppermute | solution.py:23
  249.4 22.9 %collective-permute-start.23 = (f32[64,1]{1,0:T(8,128)S(1)}, f32[64,1]{1,0:T(8,128)S(1)}, u32[]{:S(2)}, u32[]{:S(2)}) collective-permute-start(f32[64,1]{1,0:T(8,128)S(1)} %get-tuple-element.94), channel_id=1, source_target_pairs={{4,0},{8,4},{12,8},{16,12},{20,16},{24,20},{28,24},{32,28},{36,32}... | collective-permute-start | bytes 776 | tf_op jit(solution)/shard_map/ppermute | solution.py:26
  272.2 20.7 %collective-permute-start.27 = (f32[32,1]{1,0:T(8,128)}, f32[32,1]{1,0:T(8,128)S(1)}, u32[]{:S(2)}, u32[]{:S(2)}) collective-permute-start(f32[32,1]{1,0:T(8,128)} %broadcast.111), channel_id=1, source_target_pairs={{4,0},{8,4},{12,8},{16,12},{20,16},{24,20},{28,24},{32,28},{36,32}... | collective-permute-start | bytes 392 | tf_op jit(solution)/shard_map/ppermute | solution.py:26
  272.4 20.6 %collective-permute-start.24 = (f32[1,256]{1,0:T(1,128)S(1)}, f32[1,256]{1,0:T(1,128)S(1)}, u32[]{:S(2)}, u32[]{:S(2)}) collective-permute-start(f32[1,256]{1,0:T(1,128)S(1)} %broadcast.110), channel_id=1, source_target_pairs={{0,1},{1,2},{2,3},{4,5},{5,6},{6,7},{8,9},{9,10},{10,11},{12,13},{... | collective-permute-start | bytes 3080 | tf_op jit(solution)/shard_map/ppermute | solution.py:23
  277.0 16.0 %collective-permute-start.25 = (f32[1,256]{1,0:T(1,128)S(1)}, f32[1,256]{1,0:T(1,128)S(1)}, u32[]{:S(2)}, u32[]{:S(2)}) collective-permute-start(f32[1,256]{1,0:T(1,128)S(1)} %broadcast.110), channel_id=1, source_target_pairs={{1,0},{2,1},{3,2},{5,4},{6,5},{7,6},{9,8},{10,9},{11,10},{13,12},{... | collective-permute-start | bytes 3080 | tf_op jit(solution)/shard_map/ppermute | solution.py:26
  278.3 52.2 %collective-permute-start.38 = (f32[16,1]{1,0:T(8,128)S(1)}, f32[16,1]{1,0:T(8,128)S(1)}, u32[]{:S(2)}, u32[]{:S(2)}) collective-permute-start(f32[16,1]{1,0:T(8,128)S(1)} %broadcast.116), channel_id=1, source_target_pairs={{0,4},{4,8},{8,12},{12,16},{16,20},{20,24},{24,28},{28,32},{32,36}... | collective-permute-start | bytes 200 | tf_op jit(solution)/shard_map/ppermute | solution.py:23
  306.7 17.0 %collective-permute-start.32 = (f32[1,256]{1,0:T(1,128)S(1)}, f32[1,256]{1,0:T(1,128)S(1)}, u32[]{:S(2)}, u32[]{:S(2)}) collective-permute-start(f32[1,256]{1,0:T(1,128)S(1)} %get-tuple-element.123), channel_id=1, source_target_pairs={{0,1},{1,2},{2,3},{4,5},{5,6},{6,7},{8,9},{9,10},{10,11},{12,13},{... | collective-permute-start | bytes 3080 | tf_op jit(solution)/shard_map/ppermute | solution.py:23
  311.3 13.8 %collective-permute-start.33 = (f32[1,256]{1,0:T(1,128)S(1)}, f32[1,256]{1,0:T(1,128)S(1)}, u32[]{:S(2)}, u32[]{:S(2)}) collective-permute-start(f32[1,256]{1,0:T(1,128)S(1)} %get-tuple-element.124), channel_id=1, source_target_pairs={{1,0},{2,1},{3,2},{5,4},{6,5},{7,6},{9,8},{10,9},{11,10},{13,12},{... | collective-permute-start | bytes 3080 | tf_op jit(solution)/shard_map/ppermute | solution.py:26
  519.5 13.6 %collective-permute-start.96 = (f32[1,1024]{0,1:T(8,128)S(1)}, f32[1,1024]{0,1:T(8,128)S(1)}, u32[]{:S(2)}, u32[]{:S(2)}) collective-permute-start(f32[1,1024]{0,1:T(8,128)S(1)} %get-tuple-element.43), channel_id=1, source_target_pairs={{0,1},{1,2},{2,3},{4,5},{5,6},{6,7},{8,9},{9,10},{10,11},{12,13},{... | collective-permute-start | bytes 12296 | tf_op jit(solution)/shard_map/ppermute | solution.py:23
  533.8 16.6 %collective-permute-start.100 = (f32[1,1024]{0,1:T(8,128)S(1)}, f32[1,1024]{0,1:T(8,128)S(1)}, u32[]{:S(2)}, u32[]{:S(2)}) collective-permute-start(f32[1,1024]{0,1:T(8,128)S(1)} %get-tuple-element.39), channel_id=1, source_target_pairs={{0,1},{1,2},{2,3},{4,5},{5,6},{6,7},{8,9},{9,10},{10,11},{12,13},{... | collective-permute-start | bytes 12296 | tf_op jit(solution)/shard_map/ppermute | solution.py:23
  604.2 17.8 %collective-permute-start.104 = (f32[1,512]{1,0:T(1,128)S(1)}, f32[1,512]{1,0:T(1,128)S(1)}, u32[]{:S(2)}, u32[]{:S(2)}) collective-permute-start(f32[1,512]{1,0:T(1,128)S(1)} %get-tuple-element.79), channel_id=1, source_target_pairs={{0,1},{1,2},{2,3},{4,5},{5,6},{6,7},{8,9},{9,10},{10,11},{12,13},{... | collective-permute-start | bytes 6152 | tf_op jit(solution)/shard_map/ppermute | solution.py:23
  608.5 13.5 %collective-permute-start.105 = (f32[1,512]{1,0:T(1,128)S(1)}, f32[1,512]{1,0:T(1,128)S(1)}, u32[]{:S(2)}, u32[]{:S(2)}) collective-permute-start(f32[1,512]{1,0:T(1,128)S(1)} %get-tuple-element.80), channel_id=1, source_target_pairs={{1,0},{2,1},{3,2},{5,4},{6,5},{7,6},{9,8},{10,9},{11,10},{13,12},{... | collective-permute-start | bytes 6152 | tf_op jit(solution)/shard_map/ppermute | solution.py:26
  820.7 12.9 %collective-permute-start.160 = (f32[1,512]{1,0:T(1,128)S(1)}, f32[1,512]{1,0:T(1,128)S(1)}, u32[]{:S(2)}, u32[]{:S(2)}) collective-permute-start(f32[1,512]{1,0:T(1,128)S(1)} %get-tuple-element.67), channel_id=1, source_target_pairs={{0,1},{1,2},{2,3},{4,5},{5,6},{6,7},{8,9},{9,10},{10,11},{12,13},{... | collective-permute-start | bytes 6152 | tf_op jit(solution)/shard_map/ppermute | solution.py:23
  (158 other events, 1914.0 us)
where the time goes:
time: 898 us; the launch traced here: 884 us
  starting transfers between devices  472 us (53%)
  local copies, waits for them, and re-layouts  227 us (25%)
  other arithmetic  105 us (12%)
  waiting for transfers between devices  76.5 us (9%)
    ppermute x88, starting transfers between devices, padded(): lax.ppermute(lax.slice_in_dim(block, 0, width, axis=dim), axis, backward)  286 us
    ppermute x88, starting transfers between devices, padded(): lax.ppermute(lax.slice_in_dim(block, block.shape[dim] - width, None, axis...  187 us
    reshape x9, local copies, waits for them, and re-layouts, block_sum(): return field.reshape(rows // 2, 2, cols // 2, 2).sum(axis=(1, 3))  146 us
    reduce_sum x9, other arithmetic, block_sum(): return field.reshape(rows // 2, 2, cols // 2, 2).sum(axis=(1, 3))  60.4 us
    ppermute x88, waiting for transfers between devices, padded(): lax.ppermute(lax.slice_in_dim(block, block.shape[dim] - width, None, axis...  49.6 us
    reshape x3, local copies, waits for them, and re-layouts, block_max(): return field.reshape(rows // 2, 2, cols // 2, 2).max(axis=(1, 3))  48 us
    ppermute x88, waiting for transfers between devices, padded(): lax.ppermute(lax.slice_in_dim(block, 0, width, axis=dim), axis, backward)  26.9 us
    reduce_max x3, other arithmetic, block_max(): return field.reshape(rows // 2, 2, cols // 2, 2).max(axis=(1, 3))  19.7 us
  transfers between devices with their start and end apart: 176, of which 57 were waited for; matrix products, arithmetic and copies ran while one was open for 25% of the time, Pallas kernels for 0%

commit v1 on v0

v1 whole, which is shorter than its diff:
```python
import functools

import jax
import jax.numpy as jnp
from jax import lax
from jax.experimental import pallas as pl
from jax.experimental.pallas import tpu as pltpu
from jax.sharding import PartitionSpec as P

OMEGA = 0.8
MESH = pl.DeviceIdType.MESH
LANES = 128

T0, O0, N0 = 9, 24, 128
T1, O1, N1 = 5, 16, 64
T2, O2, N2 = 3, 32, 32
T3, O3, N3 = 2, 20, 16
R0, R1, R2, R3 = 176, 96, 96, 56
A0, A1, A2, A3 = (8, 168), (8, 88), (8, 88), (8, 48)
H0, H1, H2 = 16, 8, 24
DIRS = ((-1, 0), (1, 0), (0, -1), (0, 1), (-1, -1), (-1, 1), (1, -1), (1, 1))


def lanes_of(x):
    return lax.broadcasted_iota(jnp.int32, x.shape, 1)


def neighbours(src, t, count, lo, hi):
    x = src[t, lo:hi]
    lane = lanes_of(x)
    left = pltpu.roll(jnp.where(lane == LANES - 1, src[(t - 1) % count, lo:hi], x), 1, 1)
    right = pltpu.roll(jnp.where(lane == 0, src[(t + 1) % count, lo:hi], x), LANES - 1, 1)
    return x, ((src[t, lo - 1:hi - 1] + src[t, lo + 1:hi + 1]) + left) + right


def sweep(src, dst, g, b, count, lo, hi):
    for t in range(count):
        x, near = neighbours(src, t, count, lo, hi)
        dst[t, lo:hi] = (1.0 - OMEGA) * x + b[t, lo:hi] * (g[t, lo:hi] + near)


def first_sweep(dst, g, b, count, lo, hi):
    for t in range(count):
        dst[t, lo:hi] = b[t, lo:hi] * g[t, lo:hi]


def residual_of(src, dst, g, e, count, lo, hi, tiles):
    for t in range(tiles):
        x, near = neighbours(src, t, count, lo, hi)
        ee = e[t, lo:hi]
        dst[t, lo:hi] = jnp.where(ee > 0.0, (g[t, lo:hi] + near) - ee * x, 0.0)


def gather(x, index):
    return jnp.take_along_axis(x, index, axis=1, mode="promise_in_bounds")


def coarsen(src, t, tiles, lo, rows, op):
    def pair(tile):
        return op(src[tile, pl.ds(lo, rows, stride=2)], src[tile, pl.ds(lo + 1, rows, stride=2)])

    x = pair(2 * t)
    lane = lanes_of(x)
    x = op(x, pltpu.roll(x, LANES - 1, 1))
    if 2 * t + 1 < tiles:
        y = pair(2 * t + 1)
        x = jnp.where(lane % 2 == 0, x, op(y, pltpu.roll(y, 1, 1)))
        index = jnp.where(lane < LANES // 2, 2 * lane, 2 * lane - (LANES - 1))
    else:
        index = (2 * lane) % LANES
    return gather(x, index)


def correct(coarse, fine, e, count, clo, rows, lo):
    for t in range(count):
        c = coarse[t // 2, clo:clo + rows]
        lane = lanes_of(c)
        half = lane // 2
        if t == count - 1:
            index = jnp.where(lane < LANES // 2, half, LANES // 2 + half)
        else:
            index = half + (LANES // 2) * (t % 2)
        c = gather(c, index)
        for odd in range(2):
            rws = pl.ds(lo + odd, rows, stride=2)
            fine[t, rws] = fine[t, rws] + jnp.where(e[t, rws] > 0.0, c, 0.0)


def kernel(lon_count, lat_count, guide, screen, valid, tiles, out, res,
           gin, win, vin, fin, sb, e0, v0, w0, r0, vg, bb, e1, u1, r1, wa, b2, e2, gg, v2, u2, r2, b3, g3, v3, u3,
           xsb, xbb, xwa, xgg, xvg, rvg, in_sem, out_sem, send_sem, recv_sem):
    lon = lax.axis_index("lon")
    lat = lax.axis_index("lat")
    s0, b0 = sb.at[0], sb.at[1]
    v1, g1, b1 = vg.at[0], vg.at[1], bb.at[0]
    w2, a2 = wa.at[0], wa.at[1]

    loads = []
    for i, (src, dst) in enumerate(((screen, win), (valid, vin), (guide, gin))):
        for t in range(T0 - 1):
            loads.append(pltpu.make_async_copy(src.at[:, pl.ds(t * LANES, LANES)], dst.at[t], in_sem.at[i, t]))
    flag_copy = pltpu.make_async_copy(tiles, fin, in_sem.at[3, 0])
    flag_copy.start()
    for copy in loads:
        copy.start()

    def peer(d):
        return {"lat": lax.rem(lat + DIRS[d][0] + lat_count, lat_count), "lon": lax.rem(lon + DIRS[d][1] + lon_count, lon_count)}

    def exists(d):
        if DIRS[d][0] < 0:
            return lat > 0
        if DIRS[d][0] > 0:
            return lat < lat_count - 1
        return None

    def guarded(condition, fn):
        if condition is None:
            fn()
        else:
            pl.when(condition)(fn)

    barrier = pltpu.get_barrier_semaphore()
    for d in range(8):
        guarded(exists(d), lambda d=d: pl.semaphore_signal(
            barrier, inc=1, device_id=peer(d), device_id_type=MESH))

    for ref, rows, lo, hi in ((v0, R0, *A0), (w0, R0, *A0), (v1, R1, *A1), (u1, R1, *A1), (v2, R2, *A2),
                              (u2, R2, *A2), (v3, R3, *A3), (u3, R3, *A3)):
        zero = jnp.zeros((ref.shape[0], 8, LANES), jnp.float32)
        ref[:, lo - 8:lo] = zero
        ref[:, hi:hi + 8] = zero

    interior = jnp.logical_and(lat > 0, lat < lat_count - 1).astype(jnp.int32)
    pl.semaphore_wait(barrier, 5 + 3 * interior)

    def message(kind, d, src, rows_dst, land, count, first, rows, depth):
        dy, dx = DIRS[d]
        if dy < 0:
            from_rows, to_rows = pl.ds(first, depth), pl.ds(first + rows, depth)
        elif dy > 0:
            from_rows, to_rows = pl.ds(first + rows - depth, depth), pl.ds(first - depth, depth)
        else:
            from_rows = to_rows = pl.ds(first, rows)
        if dx == 0:
            src = src.at[:, pl.ds(0, count - 1), from_rows]
            dst = rows_dst.at[:, pl.ds(0, count - 1), to_rows]
        else:
            src = src.at[:, 0 if dx < 0 else count - 2, from_rows]
            dst = land.at[1 if dx < 0 else 0, :, to_rows]
        return pltpu.make_async_remote_copy(
            src_ref=src, dst_ref=dst, send_sem=send_sem.at[kind, d], recv_sem=recv_sem.at[kind, d],
            device_id=peer(d), device_id_type=MESH)

    def send(kind, *where):
        for d in range(8):
            guarded(exists(d), lambda d=d: message(kind, d, *where).start())

    def sent(kind, *where):
        for d in range(8):
            guarded(exists(d), lambda d=d: message(kind, d, *where).wait_send())

    def received(kind, *where):
        src, rows_dst, land, count, first, rows, depth = where
        for d in range(8):
            back = DIRS.index((-DIRS[d][0], -DIRS[d][1]))
            guarded(exists(back), lambda d=d: message(kind, d, *where).wait_recv())
        for outside, lo in ((lat == 0, first - depth), (lat == lat_count - 1, first + rows)):
            @pl.when(outside)
            def _():
                for k in range(rows_dst.shape[0]):
                    rows_dst[k, :, lo:lo + depth] = jnp.zeros((rows_dst.shape[1], depth, LANES), jnp.float32)
                    for side in range(2):
                        land[side, k, lo:lo + depth] = jnp.zeros((depth, LANES), jnp.float32)

    def merge(land, k, ref, count, lo, hi):
        left = land[0, k, lo:hi]
        ref[count - 1, lo:hi] = jnp.where(lanes_of(left) < LANES // 2, land[1, k, lo:hi], left)

    flag_copy.wait()
    for copy in loads:
        copy.wait()
    own = slice(O0, O0 + N0)
    for t in range(T0 - 1):
        active = vin[t].astype(jnp.float32) * fin[0, t].astype(jnp.float32)
        diag = 4.0 + win[t]
        s0[t, own] = active * gin[t]
        b0[t, own] = active * OMEGA / diag
        e0[t, own] = active * diag
        r0[t, own] = active
    msg0 = (0, sb, sb, xsb, T0, O0, N0, H0)
    send(*msg0)

    own1 = slice(O1, O1 + N1)
    for t in range(T1 - 1):
        active = coarsen(r0, t, T0 - 1, O0, N1, jnp.maximum)
        weight = coarsen(win, t, T0 - 1, 0, N1, jnp.add)
        diag = 4.0 + weight
        b1[t, own1] = active * OMEGA / diag
        e1[t, own1] = active * diag
        r1[t, own1] = active
        u1[t, own1] = weight
    msg1 = (1, bb, bb, xbb, T1, O1, N1, H1)
    send(*msg1)

    for t in range(T2 - 1):
        a2[t, O2:O2 + N2] = coarsen(r1, t, T1 - 1, O1, N2, jnp.maximum)
        w2[t, O2:O2 + N2] = coarsen(u1, t, T1 - 1, O1, N2, jnp.add)
    msg2 = (2, wa, wa, xwa, T2, O2, N2, H2)
    send(*msg2)

    def masked_inverse(x):
        return jnp.where(x > 0.0, OMEGA / jnp.where(x > 0.0, x, 1.0), 0.0)

    received(*msg0)
    for k in range(2):
        merge(xsb, k, sb.at[k], T0, *A0)
    for t in range(T0):
        for lo, hi in (A0,) if t == T0 - 1 else ((A0[0], O0), (O0 + N0, A0[1])):
            e0[t, lo:hi] = masked_inverse(b0[t, lo:hi])

    for cycle in range(2):
        g2 = gg.at[cycle, 0]
        if cycle == 0:
            first_sweep(w0, s0, b0, T0, *A0)
        else:
            sweep(v0, w0, s0, b0, T0, *A0)
        sweep(w0, v0, s0, b0, T0, *A0)
        residual_of(v0, r0, s0, e0, T0, *A0, T0)

        if cycle == 0:
            received(*msg1)
            merge(xbb, 0, b1, T1, *A1)
        for t in range(T1):
            g1[t, A1[0]:A1[1]] = jnp.where(
                b1[t, A1[0]:A1[1]] > 0.0, coarsen(r0, t, T0, A0[0], A1[1] - A1[0], jnp.add), 0.0)
        first_sweep(u1, g1, b1, T1, *A1)
        sweep(u1, v1, g1, b1, T1, *A1)
        residual_of(v1, r1, g1, e1, T1, O1, O1 + N1, T1 - 1)
        for t in range(T2 - 1):
            g2[t, O2:O2 + N2] = jnp.where(
                a2[t, O2:O2 + N2] > 0.0, coarsen(r1, t, T1 - 1, O1, N2, jnp.add), 0.0)
        msg_g = (3 + 2 * cycle, gg.at[cycle], gg.at[cycle], xgg.at[cycle], T2, O2, N2, H2)
        msg_v = (4 + 2 * cycle, vg, rvg.at[cycle], xvg.at[cycle], T1, O1, N1, H1)
        send(*msg_g)
        send(*msg_v)

        if cycle == 0:
            received(*msg2)
            for k in range(2):
                merge(xwa, k, wa.at[k], T2, *A2)
            for t in range(T2):
                lo, hi = A2
                diag = 4.0 + w2[t, lo:hi]
                b2[t, lo:hi] = a2[t, lo:hi] * OMEGA / diag
                e2[t, lo:hi] = a2[t, lo:hi] * diag
            for t in range(T3):
                lo, hi = A3
                b3[t, lo:hi] = coarsen(a2, t, T2, A2[0], hi - lo, jnp.maximum) * OMEGA / (
                    4.0 + coarsen(w2, t, T2, A2[0], hi - lo, jnp.add))
        received(*msg_g)
        merge(xgg.at[cycle], 0, g2, T2, *A2)
        first_sweep(u2, g2, b2, T2, *A2)
        sweep(u2, v2, g2, b2, T2, *A2)
        residual_of(v2, r2, g2, e2, T2, *A2, T2)
        for t in range(T3):
            lo, hi = A3
            g3[t, lo:hi] = jnp.where(b3[t, lo:hi] > 0.0, coarsen(r2, t, T2, A2[0], hi - lo, jnp.add), 0.0)
        first_sweep(v3, g3, b3, T3, *A3)
        for i in range(7):
            src, dst = (v3, u3) if i % 2 == 0 else (u3, v3)
            sweep(src, dst, g3, b3, T3, *A3)
        correct(u3, v2, e2, T2, A3[0], A3[1] - A3[0], A2[0])
        sweep(v2, u2, g2, b2, T2, *A2)
        sweep(u2, v2, g2, b2, T2, *A2)
        sent(*msg_g)

        sent(*msg_v)
        received(*msg_v)
        for k in range(2):
            for t in range(T1 - 1):
                for lo, hi in ((A1[0], O1), (O1 + N1, A1[1])):
                    vg[k, t, lo:hi] = rvg[cycle, k, t, lo:hi]
            merge(xvg.at[cycle], k, vg.at[k], T1, *A1)
        correct(v2, v1, b1, T1, O2 - 4, 40, A1[0])
        sweep(v1, u1, g1, b1, T1, *A1)
        sweep(u1, v1, g1, b1, T1, *A1)
        correct(v1, v0, e0, T0, A1[0], A1[1] - A1[0], A0[0])
        sweep(v0, w0, s0, b0, T0, *A0)
        sweep(w0, v0, s0, b0, T0, *A0)

    stores = []
    for i, (src, dst) in enumerate(((v0, out), (r0, res))):
        if i == 1:
            residual_of(v0, r0, s0, e0, T0, O0, O0 + N0, T0 - 1)
        for t in range(T0 - 1):
            stores.append(pltpu.make_async_copy(
                src.at[t, pl.ds(O0, N0)], dst.at[:, pl.ds(t * LANES, LANES)], out_sem.at[i, t]))
            stores[-1].start()
    sent(*msg0)
    sent(*msg1)
    sent(*msg2)
    for copy in stores:
        copy.wait()


def solution(mesh):
    def body(guide, screen, valid, tiles):
        def vmem(*shape):
            return pltpu.VMEM(shape + (LANES,), jnp.float32)

        block = jax.ShapeDtypeStruct(guide.shape, jnp.float32)
        return pl.pallas_call(
            functools.partial(kernel, mesh.shape["lon"], mesh.shape["lat"]),
            out_shape=(block, block),
            in_specs=[pl.BlockSpec(memory_space=pl.ANY)] * 4,
            out_specs=(pl.BlockSpec(memory_space=pl.ANY),) * 2,
            scratch_shapes=[
                vmem(T0 - 1, N0), vmem(T0 - 1, N0), pltpu.VMEM((T0 - 1, N0, LANES), jnp.int32),
                pltpu.SMEM((1, T0 - 1), jnp.int32),
                vmem(2, T0, R0), vmem(T0, R0), vmem(T0, R0), vmem(T0, R0), vmem(T0, R0),
                vmem(2, T1, R1), vmem(1, T1, R1), vmem(T1, R1), vmem(T1, R1), vmem(T1, R1),
                vmem(2, T2, R2), vmem(T2, R2), vmem(T2, R2), vmem(2, 1, T2, R2), vmem(T2, R2), vmem(T2, R2),
                vmem(T2, R2),
                vmem(T3, R3), vmem(T3, R3), vmem(T3, R3), vmem(T3, R3),
                vmem(2, 2, R0), vmem(2, 1, R1), vmem(2, 2, R2), vmem(2, 2, 1, R2), vmem(2, 2, 2, R1),
                vmem(2, 2, T1, R1),
                pltpu.SemaphoreType.DMA((4, T0 - 1)), pltpu.SemaphoreType.DMA((2, T0 - 1)),
                pltpu.SemaphoreType.DMA((7, 8)), pltpu.SemaphoreType.DMA((7, 8)),
            ],
            compiler_params=pltpu.CompilerParams(
                collective_id=0, has_side_effects=True, vmem_limit_bytes=48 * 1024 * 1024),
        )(guide, screen, valid, tiles)

    spec = P("lat", "lon")
    return jax.shard_map(
        body, mesh=mesh, in_specs=(spec,) * 4, out_specs=(spec,) * 2, check_vma=False)
```

time: 898 us -> 40.7 us (0.05)
  the two profiles are of different devices: /device:TPU:0 before, /device:TPU:1 now
where the time goes in v1:
time: 40.7 us; the launch traced here: 40.4 us
  Pallas kernels  34.4 us (85%)
  local copies, waits for them, and re-layouts  5.36 us (13%)
  between operations  0.65 us (2%)
    pallas_call x1, Pallas kernels, body(): pl.pallas_call(functools.partial(kernel, mesh.shape['lon'], mesh.shape['l...  34.4 us
    unnamed x10, local copies, waits for them, and re-layouts  5.36 us

profile of v1, /device:TPU:1, one launch (start us, length us, event | category | flops | bytes accessed | tf_op | source)
XLA Modules:
  0.0 40.4 jit_solution(5457856638032866219)
XLA Ops:
  0.6 0.0 copy-start
  0.6 1.0 %copy-done = f32[128,1024]{1,0:T(8,128)S(1)} copy-done((f32[128,1024]{1,0:T(8,128)S(1)}, f32[128,1024]{1,0:T(8,128)}, u32[]{:S(2)}) %copy-start) | copy-done | bytes 524312
  1.7 0.0 copy-start.1
  1.7 1.0 %copy-done.1 = f32[128,1024]{1,0:T(8,128)S(1)} copy-done((f32[128,1024]{1,0:T(8,128)S(1)}, f32[128,1024]{1,0:T(8,128)}, u32[]{:S(2)}) %copy-start.1) | copy-done | bytes 524312
  2.7 0.0 copy-start.2
  2.7 1.0 %copy-done.2 = s32[128,1024]{1,0:T(8,128)S(1)} copy-done((s32[128,1024]{1,0:T(8,128)S(1)}, s32[128,1024]{1,0:T(8,128)}, u32[]{:S(2)}) %copy-start.2) | copy-done | bytes 524312
  3.8 0.0 copy-start.3
  3.8 0.7 %copy-done.3 = s32[1,8]{1,0:T(1,128)S(1)} copy-done((s32[1,8]{1,0:T(1,128)S(1)}, s32[1,8]{1,0:T(1,128)}, u32[]{:S(2)}) %copy-start.3) | copy-done | bytes 56
  4.4 34.4 %shard_map.59 = (f32[128,1024]{1,0:T(8,128)S(1)}, f32[128,1024]{1,0:T(8,128)S(1)}) custom-call(f32[128,1024]{1,0:T(8,128)S(1)} %copy-done, f32[128,1024]{1,0:T(8,128)S(1)} %copy-done.1, s32[128,1024]{1,0:T(8,128)S(1)} %copy-done.2, s32[1,8]{1,0:T(1,128)S(1)} %copy-done.3), custom_call_target="tpu_custom_call" | custom-call | tf_op jit(solution)/shard_map/pallas_call | solution.py:313
  38.9 0.8 %copy.8 = f32[128,1024]{1,0:T(8,128)} copy(f32[128,1024]{1,0:T(8,128)S(1)} %get-tuple-element.4) | data formatting | bytes 1048576
  39.7 0.8 %copy.9 = f32[128,1024]{1,0:T(8,128)} copy(f32[128,1024]{1,0:T(8,128)S(1)} %get-tuple-element.5) | data formatting | bytes 1048576
Async XLA Ops:
  0.6 1.0 %copy-start = (f32[128,1024]{1,0:T(8,128)S(1)}, f32[128,1024]{1,0:T(8,128)}, u32[]{:S(2)}) copy-start(f32[128,1024]{1,0:T(8,128)} %guide.1) | copy-start | bytes 1572868
  1.7 1.0 %copy-start.1 = (f32[128,1024]{1,0:T(8,128)S(1)}, f32[128,1024]{1,0:T(8,128)}, u32[]{:S(2)}) copy-start(f32[128,1024]{1,0:T(8,128)} %screen.1) | copy-start | bytes 1572868
  2.7 1.0 %copy-start.2 = (s32[128,1024]{1,0:T(8,128)S(1)}, s32[128,1024]{1,0:T(8,128)}, u32[]{:S(2)}) copy-start(s32[128,1024]{1,0:T(8,128)} %valid.1) | copy-start | bytes 1572868
  3.8 0.7 %copy-start.3 = (s32[1,8]{1,0:T(1,128)S(1)}, s32[1,8]{1,0:T(1,128)}, u32[]{:S(2)}) copy-start(s32[1,8]{1,0:T(1,128)} %tiles.1) | copy-start | bytes 100

commit v2 on v1

--- a/solution.py
+++ b/solution.py
@@ -100,9 +100,6 @@
         for t in range(T0 - 1):
             loads.append(pltpu.make_async_copy(src.at[:, pl.ds(t * LANES, LANES)], dst.at[t], in_sem.at[i, t]))
     flag_copy = pltpu.make_async_copy(tiles, fin, in_sem.at[3, 0])
-    flag_copy.start()
-    for copy in loads:
-        copy.start()
 
     def peer(d):
         return {"lat": lax.rem(lat + DIRS[d][0] + lat_count, lat_count), "lon": lax.rem(lon + DIRS[d][1] + lon_count, lon_count)}
@@ -125,6 +122,9 @@
         guarded(exists(d), lambda d=d: pl.semaphore_signal(
             barrier, inc=1, device_id=peer(d), device_id_type=MESH))
 
+    flag_copy.start()
+    for copy in loads:
+        copy.start()
     for ref, rows, lo, hi in ((v0, R0, *A0), (w0, R0, *A0), (v1, R1, *A1), (u1, R1, *A1), (v2, R2, *A2),
                               (u2, R2, *A2), (v3, R3, *A3), (u3, R3, *A3)):
         zero = jnp.zeros((ref.shape[0], 8, LANES), jnp.float32)
@@ -304,15 +304,24 @@
         copy.wait()
 
 
+def store(a, b, out, res, sem):
+    copies = [pltpu.make_async_copy(x, y, sem.at[i]) for i, (x, y) in enumerate(((a, out), (b, res)))]
+    for copy in copies:
+        copy.start()
+    for copy in copies:
+        copy.wait()
+
+
 def solution(mesh):
     def body(guide, screen, valid, tiles):
         def vmem(*shape):
             return pltpu.VMEM(shape + (LANES,), jnp.float32)
 
-        block = jax.ShapeDtypeStruct(guide.shape, jnp.float32)
-        return pl.pallas_call(
+        guide, screen, valid, tiles = [
+            pltpu.with_memory_space_constraint(x, pltpu.HBM) for x in (guide, screen, valid, tiles)]
+        pair = pl.pallas_call(
             functools.partial(kernel, mesh.shape["lon"], mesh.shape["lat"]),
-            out_shape=(block, block),
+            out_shape=(pltpu.VMEM(guide.shape, jnp.float32),) * 2,
             in_specs=[pl.BlockSpec(memory_space=pl.ANY)] * 4,
             out_specs=(pl.BlockSpec(memory_space=pl.ANY),) * 2,
             scratch_shapes=[
@@ -331,6 +340,14 @@
             compiler_params=pltpu.CompilerParams(
                 collective_id=0, has_side_effects=True, vmem_limit_bytes=48 * 1024 * 1024),
         )(guide, screen, valid, tiles)
+        pair = [pltpu.with_memory_space_constraint(x, pltpu.VMEM) for x in pair]
+        return pl.pallas_call(
+            store,
+            out_shape=(pltpu.HBM(guide.shape, jnp.float32),) * 2,
+            in_specs=[pl.BlockSpec(memory_space=pl.ANY)] * 2,
+            out_specs=(pl.BlockSpec(memory_space=pltpu.HBM),) * 2,
+            scratch_shapes=[pltpu.SemaphoreType.DMA((2,))],
+        )(*pair)
 
     spec = P("lat", "lon")
     return jax.shard_map(

time: 40.7 us -> 36.1 us (0.89)
  local copies, waits for them, and re-layouts: 5.36 us -> 0 us
  Pallas kernels: 34.4 us -> 35.3 us
    unnamed x10 -> x0, local copies, waits for them, and re-layouts: 5.36 us -> none
    pallas_call x0 -> x1, Pallas kernels: none -> 0.99 us  [body(): pl.pallas_call(store, out_shape=(pltpu.HBM(guide.shape, jnp.float32),) *...]
where the time goes in v2:
time: 36.1 us; the launch traced here: 35.9 us
  Pallas kernels  35.3 us (98%)
  between operations  0.64 us (2%)
    pallas_call x1, Pallas kernels, body(): pl.pallas_call(functools.partial(kernel, mesh.shape['lon'], mesh.shape['l...  34.3 us
    pallas_call x1, Pallas kernels, body(): pl.pallas_call(store, out_shape=(pltpu.HBM(guide.shape, jnp.float32),) *...  0.99 us

profile of v2, /device:TPU:1, one launch (start us, length us, event | category | flops | bytes accessed | tf_op | source)
XLA Modules:
  0.0 35.9 jit_solution(2734198988732161746)
XLA Ops:
  0.6 34.3 %shard_map.59 = (f32[128,1024]{1,0:T(8,128)S(1)}, f32[128,1024]{1,0:T(8,128)S(1)}) custom-call(f32[128,1024]{1,0:T(8,128)} %guide.1, f32[128,1024]{1,0:T(8,128)} %screen.1, s32[128,1024]{1,0:T(8,128)} %valid.1, s32[1,8]{1,0:T(1,128)} %tiles.1), custom_call_target="tpu_custom_call" | custom-call | tf_op jit(solution)/shard_map/pallas_call | solution.py:322
  34.9 1.0 %shard_map.60 = (f32[128,1024]{1,0:T(8,128)}, f32[128,1024]{1,0:T(8,128)}) custom-call(f32[128,1024]{1,0:T(8,128)S(1)} %get-tuple-element.4.a, f32[128,1024]{1,0:T(8,128)S(1)} %get-tuple-element.5.b), custom_call_target="tpu_custom_call" | custom-call | tf_op jit(solution)/shard_map/pallas_call | solution.py:344

commit v3 on v0

v3 whole, which is shorter than its diff:
```python
import functools

import jax
import jax.numpy as jnp
from jax import lax
from jax.experimental import pallas as pl
from jax.experimental.pallas import tpu as pltpu
from jax.sharding import PartitionSpec as P

OMEGA = 0.8
MESH = pl.DeviceIdType.MESH
LANES = 128
HALF = LANES // 2

P0, P1, P2, P3 = 4, 2, 1, 1
T0, T1, T2, T3 = 3, 3, 3, 2
O0, O1, O2, O3 = 24, 16, 32, 20
N0, N1, N2, N3 = 128, 64, 32, 16
R0, R1, R2, R3 = 176, 96, 96, 56
A0, B0, A1, A2, A3 = (8, 168), (16, 160), (8, 88), (8, 88), (8, 48)
H0, H1, H2 = 16, 8, 24
OWN = 8
DIRS = ((-1, 0), (1, 0), (0, -1), (0, 1), (-1, -1), (-1, 1), (1, -1), (1, 1))


def lanes_of(x):
    return lax.broadcasted_iota(jnp.int32, x.shape, 1)


def gather(x, index):
    return jnp.take_along_axis(x, index, axis=1, mode="promise_in_bounds")


def barrel(tiles, lane):
    odd, high = (lane & 32) != 0, lane >= HALF
    half = [jnp.where(odd, tiles[(i + 1) % 4], tiles[i]) for i in range(4)]
    return [jnp.where(high, half[(i + 2) % 4], half[i]) for i in range(4)]


def split_phases(sources, mid, rows, store):
    for t, src in enumerate(sources):
        x = src(slice(0, rows))
        lane = lanes_of(x)
        mid[t, 0:rows] = gather(x, ((lane & 31) << 2) + (((lane >> 5) + (4 - t)) & 3))
    for row in range(0, rows, 16):
        part = slice(row, row + 16)
        tiles = [mid[t, part] for t in range(4)]
        mixed = barrel(tiles, lanes_of(tiles[0]))
        store(0, part, mixed[0])
        for p in range(1, 4):
            store(p, part, pltpu.roll(mixed[4 - p], LANES - 32 * p, 1))


def join_phases(sources, mid, rows, stores):
    for row in range(0, rows, 16):
        part = slice(row, row + 16)
        phases = [src(part) for src in sources]
        placed = [phases[0]] + [pltpu.roll(phases[p], 32 * p, 1) for p in range(1, 4)]
        mixed = barrel(placed, lanes_of(placed[0]))
        for t in range(4):
            mid[t, part] = mixed[(4 - t) % 4]
    for t, store in enumerate(stores):
        x = mid[t, 0:rows]
        lane = lanes_of(x)
        store(gather(x, (((lane + t) & 3) << 5) + (lane >> 2)))


def neighbours(src, i, phases, count, lo, hi):
    t, p = i // phases, i % phases
    x = src[i, lo:hi]
    lane = lanes_of(x)
    if p > 0:
        left = src[i - 1, lo:hi]
    else:
        last = phases - 1
        left = pltpu.roll(jnp.where(
            lane == LANES - 1, src[((t - 1) % count) * phases + last, lo:hi], src[t * phases + last, lo:hi]), 1, 1)
    if p < phases - 1:
        right = src[i + 1, lo:hi]
    else:
        right = pltpu.roll(jnp.where(
            lane == 0, src[((t + 1) % count) * phases, lo:hi], src[t * phases, lo:hi]), LANES - 1, 1)
    return x, ((src[i, lo - 1:hi - 1] + src[i, lo + 1:hi + 1]) + left) + right


def sweep(src, dst, g, b, phases, count, lo, hi):
    for i in range(phases * count):
        x, near = neighbours(src, i, phases, count, lo, hi)
        dst[i, lo:hi] = (1.0 - OMEGA) * x + b[i, lo:hi] * (g[i, lo:hi] + near)


def first_sweep(dst, g, b, planes, lo, hi):
    for i in range(planes):
        dst[i, lo:hi] = b[i, lo:hi] * g[i, lo:hi]


def residual_of(src, g, e, i, phases, count, lo, hi):
    x, near = neighbours(src, i, phases, count, lo, hi)
    ee = e[i, lo:hi]
    return jnp.where(ee > 0.0, (g[i, lo:hi] + near) - ee * x, 0.0)


def rows_op(src, i, lo, rows, op):
    return op(src[i, pl.ds(lo, rows, stride=2)], src[i, pl.ds(lo + 1, rows, stride=2)])


def restrict(src, g, e, phases, count, planes, lo, hi, tmp, out, active, tlo, olo, rows):
    for i in range(planes):
        tmp[i, lo:hi] = residual_of(src, g, e, 2 * i, phases, count, lo, hi) + residual_of(
            src, g, e, 2 * i + 1, phases, count, lo, hi)
    for i in range(planes):
        out[i, olo:olo + rows] = jnp.where(
            active[i, olo:olo + rows] > 0.0, rows_op(tmp, i, tlo, rows, jnp.add), 0.0)


def coarsen(src, i, lo, rows, op):
    return op(rows_op(src, 2 * i, lo, rows, op), rows_op(src, 2 * i + 1, lo, rows, op))


def correct(coarse, fine, b, planes, clo, rows, lo, tmp):
    hi = lo + 2 * rows
    for i in range(planes):
        c = coarse[i, clo:clo + rows]
        tmp[i, pl.ds(lo, rows, stride=2)] = c
        tmp[i, pl.ds(lo + 1, rows, stride=2)] = c
    for i in range(2 * planes):
        fine[i, lo:hi] = fine[i, lo:hi] + jnp.where(b[i, lo:hi] > 0.0, tmp[i // 2, lo:hi], 0.0)


def pack(src, t, lo, rows, op):
    x = rows_op(src, 2 * t, lo, rows, op)
    lane = lanes_of(x)
    x = op(x, pltpu.roll(x, LANES - 1, 1))
    if 2 * t + 1 < T2:
        y = rows_op(src, 2 * t + 1, lo, rows, op)
        x = jnp.where((lane & 1) == 0, x, op(y, pltpu.roll(y, 1, 1)))
        index = jnp.where(lane < HALF, 2 * lane, 2 * lane - (LANES - 1))
    else:
        index = (2 * lane) & (LANES - 1)
    return gather(x, index)


def unpack(coarse, fine, b, clo, rows, lo, tmp):
    hi = lo + 2 * rows
    for t in range(T2):
        c = coarse[t // 2, clo:clo + rows]
        lane = lanes_of(c)
        if t == T2 - 1:
            index = (lane >> 1) + jnp.where(lane < HALF, 0, HALF)
        else:
            index = (lane >> 1) + HALF * (t % 2)
        c = gather(c, index)
        tmp[t, pl.ds(lo, rows, stride=2)] = c
        tmp[t, pl.ds(lo + 1, rows, stride=2)] = c
    for t in range(T2):
        fine[t, lo:hi] = fine[t, lo:hi] + jnp.where(b[t, lo:hi] > 0.0, tmp[t, lo:hi], 0.0)


def masked_inverse(x):
    return jnp.where(x > 0.0, OMEGA / jnp.where(x > 0.0, x, 1.0), 0.0)


def kernel(lon_count, lat_count, guide, screen, valid, tiles, out, res,
           gin, win, vin, fin, nat, mid, s0, b0, e0, v0, w0, tmp, vg, bb, e1, u1, wa, b2, e2, gg, v2, u2, r2, b3, g3, v3, u3,
           xbb, xwa, rvg, in_sem, out_sem, send_sem, recv_sem):
    lon = lax.axis_index("lon")
    lat = lax.axis_index("lat")
    v1, g1, b1 = vg.at[0], vg.at[1], bb.at[0]
    w2, a2 = wa.at[0], wa.at[1]
    n0, n1, n2, n3 = P0 * T0, P1 * T1, P2 * T2, P3 * T3

    def peer(d):
        return {"lat": lax.rem(lat + DIRS[d][0] + lat_count, lat_count),
                "lon": lax.rem(lon + DIRS[d][1] + lon_count, lon_count)}

    def exists(dy):
        return lat > 0 if dy < 0 else lat < lat_count - 1 if dy > 0 else None

    def guarded(condition, fn):
        if condition is None:
            fn()
        else:
            pl.when(condition)(fn)

    barrier = pltpu.get_barrier_semaphore()
    for d in range(8):
        guarded(exists(DIRS[d][0]), lambda d=d: pl.semaphore_signal(
            barrier, inc=1, device_id=peer(d), device_id_type=MESH))

    loads = [pltpu.make_async_copy(src, dst, in_sem.at[i]) for i, (src, dst) in enumerate((
        (valid, vin), (screen, win), (guide, gin), (tiles, fin)))]
    for copy in loads:
        copy.start()

    for ref, lo, hi in ((v0, *A0), (w0, *A0), (v1, *A1), (u1, *A1), (v2, *A2), (u2, *A2), (v3, *A3), (u3, *A3)):
        zero = jnp.zeros((ref.shape[0], 8, LANES), jnp.float32)
        ref[:, lo - 8:lo] = zero
        ref[:, hi:hi + 8] = zero

    def copy_of(message, d):
        kind, parts = message
        src, dst = parts[d]
        return pltpu.make_async_remote_copy(
            src_ref=src, dst_ref=dst, send_sem=send_sem.at[kind, d], recv_sem=recv_sem.at[kind, d],
            device_id=peer(d), device_id_type=MESH)

    def send(message):
        for d in message[1]:
            guarded(exists(DIRS[d][0]), lambda d=d: copy_of(message, d).start())

    def sent(message):
        for d in message[1]:
            guarded(exists(DIRS[d][0]), lambda d=d: copy_of(message, d).wait_send())

    def received(message):
        for d in message[1]:
            guarded(exists(-DIRS[d][0]), lambda d=d: copy_of(message, d).wait_recv())

    def clear(refs, above, below):
        for edge, rows in ((lat == 0, above), (lat == lat_count - 1, below)):
            @pl.when(edge)
            def _():
                for ref in refs:
                    zero = jnp.zeros((rows[1] - rows[0], LANES), jnp.float32)
                    for i in range(ref.shape[0]):
                        ref[i, rows[0]:rows[1]] = zero

    def row_spans(dy, first, rows, depth, skip=0):
        if dy < 0:
            return pl.ds(first + skip, depth), pl.ds(first + rows + skip, depth)
        if dy > 0:
            return pl.ds(first + rows - depth - skip, depth), pl.ds(first - depth - skip, depth)
        return (pl.ds(first, rows),) * 2

    first_parts, far_parts = {}, {}
    for d, (dy, dx) in enumerate(DIRS):
        if dx == 0:
            own = pl.ds(0, OWN)
            for parts, skip in ((first_parts, 0), (far_parts, 8)):
                a, b = row_spans(dy, H0, N0, 8, skip)
                parts[d] = nat.at[:, own, a], nat.at[:, own, b]
        else:
            a, b = row_spans(dy, H0, N0, H0)
            mine, theirs = (0, OWN) if dx < 0 else (OWN - 2, OWN + 2)
            first_parts[d] = nat.at[:, pl.ds(mine, 2), a], nat.at[:, pl.ds(theirs, 2), b]
    first_message, far_message = (0, first_parts), (1, far_parts)

    def coarse_parts(ref, land, phases, first, rows, depth):
        parts = {}
        for d, (dy, dx) in enumerate(DIRS):
            a, b = row_spans(dy, first, rows, depth)
            if dx == 0:
                own = pl.ds(0, 2 * phases)
                parts[d] = ref.at[:, own, a], ref.at[:, own, b]
            else:
                mine, side = (0, 1) if dx < 0 else (phases, 0)
                parts[d] = ref.at[:, pl.ds(mine, phases), a], land.at[side, :, :, b]
        return parts

    def row_parts(src, dst, first, rows, depth):
        parts = {}
        for d in range(2):
            a, b = row_spans(DIRS[d][0], first, rows, depth)
            parts[d] = src.at[..., a, :], dst.at[..., b, :]
        return parts

    def merge(land, k, ref, phases, lo, hi):
        for p in range(phases):
            left = land[0, k, p, lo:hi]
            ref[2 * phases + p, lo:hi] = jnp.where(lanes_of(left) < HALF, land[1, k, p, lo:hi], left)

    for copy in loads:
        copy.wait()
    for t in range(OWN):
        cols = slice(t * LANES, (t + 1) * LANES)
        active = vin[:, cols].astype(jnp.float32) * fin[0, t].astype(jnp.float32)
        nat[0, t, H0:H0 + N0] = active * gin[:, cols]
        nat[1, t, H0:H0 + N0] = active * OMEGA / (4.0 + win[:, cols])
    interior = jnp.logical_and(lat > 0, lat < lat_count - 1).astype(jnp.int32)
    pl.semaphore_wait(barrier, 5 + 3 * interior)
    send(first_message)
    send(far_message)

    def arrange(t, lo, hi):
        for k, ref in enumerate((s0, b0)):
            def store(p, part, x, ref=ref):
                ref[P0 * t + p, lo + O0 - H0 + part.start:lo + O0 - H0 + part.stop] = x

            split_phases([lambda part, j=j: nat[k, 4 * t + j, lo + part.start:lo + part.stop] for j in range(4)],
                         mid.at[k], hi - lo, store)

    def columns(t):
        return slice(t * LANES, (t + 1) * LANES)

    for t in range(2):
        arrange(t, H0, H0 + N0)

        def store_weight(p, part, x):
            w0[P0 * t + p, part.start + O0:part.stop + O0] = x

        split_phases([lambda part, j=j: win[part, columns(4 * t + j)] for j in range(4)], mid.at[0], N0, store_weight)
    own = slice(O0, O0 + N0)
    for i in range(2 * P0):
        on = b0[i, own] > 0.0
        e0[i, own] = jnp.where(on, 4.0 + w0[i, own], 0.0)
        v0[i, own] = jnp.where(on, 1.0, 0.0)

    own = slice(O1, O1 + N1)
    for i in range(2 * P1):
        active = coarsen(v0, i, O0, N1, jnp.maximum)
        weight = coarsen(w0, i, O0, N1, jnp.add)
        diag = 4.0 + weight
        b1[i, own] = active * OMEGA / diag
        v1[i, own] = active
        u1[i, own] = weight
    message1 = (2, coarse_parts(bb, xbb, P1, O1, N1, H1))
    send(message1)

    for i in range(2 * P2):
        w2[i, O2:O2 + N2] = coarsen(u1, i, O1, N2, jnp.add)
        a2[i, O2:O2 + N2] = coarsen(v1, i, O1, N2, jnp.maximum)
    message2 = (3, coarse_parts(wa, xwa, P2, O2, N2, H2))
    send(message2)

    received(first_message)
    received(far_message)
    clear((nat.at[0], nat.at[1]), (0, H0), (H0 + N0, 2 * H0 + N0))
    for t in range(T0):
        for lo, hi in ((0, 2 * H0 + N0),) if t == T0 - 1 else ((0, H0), (H0 + N0, 2 * H0 + N0)):
            arrange(t, lo, hi)
            for i in range(P0 * t, P0 * t + P0):
                e0[i, lo + 8:hi + 8] = masked_inverse(b0[i, lo + 8:hi + 8])

    for cycle in range(2):
        rows0 = A0 if cycle == 0 else B0
        g2 = gg.at[cycle]
        if cycle == 0:
            first_sweep(w0, s0, b0, n0, *rows0)
        else:
            sweep(v0, w0, s0, b0, P0, T0, *rows0)
        sweep(w0, v0, s0, b0, P0, T0, *rows0)

        if cycle == 0:
            received(message1)
            clear((bb.at[0], xbb.at[0, 0], xbb.at[1, 0]), (O1 - H1, O1), (O1 + N1, O1 + N1 + H1))
            merge(xbb, 0, b1, P1, *A1)
            for i in range(n1):
                e1[i, A1[0]:A1[1]] = masked_inverse(b1[i, A1[0]:A1[1]])
        restrict(v0, s0, e0, P0, T0, n1, *B0, tmp, g1, b1, A0[0], A1[0], A1[1] - A1[0])
        first_sweep(u1, g1, b1, n1, *A1)
        sweep(u1, v1, g1, b1, P1, T1, *A1)
        if cycle == 0:
            received(message2)
            clear((w2, a2, xwa.at[0, 0], xwa.at[0, 1], xwa.at[1, 0], xwa.at[1, 1]),
                  (O2 - H2, O2), (O2 + N2, O2 + N2 + H2))
            for k in range(2):
                merge(xwa, k, wa.at[k], P2, *A2)
        restrict(v1, g1, e1, P1, T1, n2, O1, O1 + N1, tmp, g2, a2, O1, O2, N2)
        message_g = (4 + cycle, row_parts(g2, g2, O2, N2, H2))
        message_v = (6 + cycle, row_parts(vg, rvg.at[cycle], O1, N1, H1))
        send(message_g)
        send(message_v)

        if cycle == 0:
            lo, hi = A2
            for t in range(n2):
                diag = 4.0 + w2[t, lo:hi]
                b2[t, lo:hi] = a2[t, lo:hi] * OMEGA / diag
                e2[t, lo:hi] = a2[t, lo:hi] * diag
            lo, hi = A3
            for t in range(n3):
                b3[t, lo:hi] = pack(a2, t, A2[0], hi - lo, jnp.maximum) * OMEGA / (
                    4.0 + pack(w2, t, A2[0], hi - lo, jnp.add))
        received(message_g)
        clear((g2,), (O2 - H2, O2), (O2 + N2, O2 + N2 + H2))
        first_sweep(u2, g2, b2, n2, *A2)
        sweep(u2, v2, g2, b2, P2, T2, *A2)
        for t in range(n2):
            r2[t, A2[0]:A2[1]] = residual_of(v2, g2, e2, t, P2, T2, *A2)
        lo, hi = A3
        for t in range(n3):
            g3[t, lo:hi] = jnp.where(b3[t, lo:hi] > 0.0, pack(r2, t, A2[0], hi - lo, jnp.add), 0.0)
        first_sweep(v3, g3, b3, n3, *A3)
        for i in range(7):
            src, dst = (v3, u3) if i % 2 == 0 else (u3, v3)
            sweep(src, dst, g3, b3, P3, T3, *A3)
        unpack(u3, v2, b2, A3[0], hi - lo, A2[0], tmp)
        sweep(v2, u2, g2, b2, P2, T2, *A2)
        sweep(u2, v2, g2, b2, P2, T2, *A2)

        sent(message_g)
        sent(message_v)
        received(message_v)
        clear((rvg.at[cycle, 0], rvg.at[cycle, 1]), (O1 - H1, O1), (O1 + N1, O1 + N1 + H1))
        for k in range(2):
            for i in range(n1):
                for lo, hi in ((A1[0], O1), (O1 + N1, A1[1])):
                    vg[k, i, lo:hi] = rvg[cycle, k, i, lo:hi]
        correct(v2, v1, b1, n2, O2 - 4, (A1[1] - A1[0]) // 2, A1[0], tmp)
        sweep(v1, u1, g1, b1, P1, T1, *A1)
        sweep(u1, v1, g1, b1, P1, T1, *A1)
        correct(v1, v0, b0, n1, A1[0], A1[1] - A1[0], A0[0], tmp)
        sweep(v0, w0, s0, b0, P0, T0, *rows0)
        sweep(w0, v0, s0, b0, P0, T0, *rows0)

    stores = []
    for k, (stage, dst) in enumerate(((gin, out), (win, res))):
        if k == 1:
            for i in range(2 * P0):
                w0[i, O0:O0 + N0] = residual_of(v0, s0, e0, i, P0, T0, O0, O0 + N0)
        src = w0 if k == 1 else v0
        for t in range(2):
            def store_tile(j, x):
                stage[:, columns(4 * t + j)] = x

            join_phases([lambda part, p=p: src[P0 * t + p, part.start + O0:part.stop + O0] for p in range(P0)],
                        mid.at[t], N0, [functools.partial(store_tile, j) for j in range(4)])
        stores.append(pltpu.make_async_copy(stage, dst, out_sem.at[k]))
        stores[-1].start()
    for message in (first_message, far_message, message1, message2):
        sent(message)
    for copy in stores:
        copy.wait()


def store(a, b, out, res, sem):
    copies = [pltpu.make_async_copy(x, y, sem.at[i]) for i, (x, y) in enumerate(((a, out), (b, res)))]
    for copy in copies:
        copy.start()
    for copy in copies:
        copy.wait()


def solution(mesh):
    def body(guide, screen, valid, tiles):
        def vmem(*shape):
            return pltpu.VMEM(shape + (LANES,), jnp.float32)

        n0, n1, n2, n3 = P0 * T0, P1 * T1, P2 * T2, P3 * T3
        block = guide.shape
        guide, screen, valid, tiles = [
            pltpu.with_memory_space_constraint(x, pltpu.HBM) for x in (guide, screen, valid, tiles)]
        pair = pl.pallas_call(
            functools.partial(kernel, mesh.shape["lon"], mesh.shape["lat"]),
            out_shape=(pltpu.VMEM(block, jnp.float32),) * 2,
            in_specs=[pl.BlockSpec(memory_space=pl.ANY)] * 4,
            out_specs=(pl.BlockSpec(memory_space=pl.ANY),) * 2,
            scratch_shapes=[
                pltpu.VMEM(block, jnp.float32), pltpu.VMEM(block, jnp.float32), pltpu.VMEM(block, jnp.int32),
                pltpu.SMEM((1, OWN), jnp.int32),
                vmem(2, OWN + 4, N0 + 2 * H0), vmem(2, 4, N0 + 2 * H0), vmem(n0, R0), vmem(n0, R0), vmem(n0, R0), vmem(n0, R0), vmem(n0, R0),
                vmem(n1, R0),
                vmem(2, n1, R1), vmem(1, n1, R1), vmem(n1, R1), vmem(n1, R1),
                vmem(2, n2, R2), vmem(n2, R2), vmem(n2, R2), vmem(2, n2, R2), vmem(n2, R2), vmem(n2, R2), vmem(n2, R2),
                vmem(n3, R3), vmem(n3, R3), vmem(n3, R3), vmem(n3, R3),
                vmem(2, 1, P1, R1), vmem(2, 2, P2, R2), vmem(2, 2, n1, R1),
                pltpu.SemaphoreType.DMA((4,)), pltpu.SemaphoreType.DMA((2,)),
                pltpu.SemaphoreType.DMA((8, 8)), pltpu.SemaphoreType.DMA((8, 8)),
            ],
            compiler_params=pltpu.CompilerParams(
                collective_id=0, has_side_effects=True, vmem_limit_bytes=48 * 1024 * 1024),
        )(guide, screen, valid, tiles)
        pair = [pltpu.with_memory_space_constraint(x, pltpu.VMEM) for x in pair]
        return pl.pallas_call(
            store,
            out_shape=(pltpu.HBM(block, jnp.float32),) * 2,
            in_specs=[pl.BlockSpec(memory_space=pl.ANY)] * 2,
            out_specs=(pl.BlockSpec(memory_space=pltpu.HBM),) * 2,
            scratch_shapes=[pltpu.SemaphoreType.DMA((2,))],
        )(*pair)

    spec = P("lat", "lon")
    return jax.shard_map(
        body, mesh=mesh, in_specs=(spec,) * 4, out_specs=(spec,) * 2, check_vma=False)
```

time: 898 us -> 32.6 us (0.04); the launches traced: 884 us -> 32.4 us
  starting transfers between devices: 472 us -> 0 us
  local copies, waits for them, and re-layouts: 227 us -> 0 us
  other arithmetic: 105 us -> 0 us
  waiting for transfers between devices: 76.5 us -> 0 us
  Pallas kernels: 0 us -> 31.8 us
    ppermute x176 -> x0, starting transfers between devices: 472 us -> none  [the longest x88 286 us: padded(): lax.ppermute(lax.slice_in_dim(block, 0, width, axis=dim), axis, backward)]
    reshape x26 -> x0, local copies, waits for them, and re-layouts: 204 us -> none  [the longest x9 146 us: block_sum(): return field.reshape(rows // 2, 2, cols // 2, 2).sum(axis=(1, 3))]
    ppermute x176 -> x0, waiting for transfers between devices: 76.5 us -> none  [the longest x88 49.6 us: padded(): lax.ppermute(lax.slice_in_dim(block, block.shape[dim] - width, None, axis...]
    reduce_sum x9 -> x0, other arithmetic: 60.4 us -> none  [block_sum(): return field.reshape(rows // 2, 2, cols // 2, 2).sum(axis=(1, 3))]
    pallas_call x0 -> x2, Pallas kernels: none -> 31.8 us  [the longest x1 30.8 us: body(): pl.pallas_call(functools.partial(kernel, mesh.shape['lon'], mesh.shape['l...]
    reduce_max x3 -> x0, other arithmetic: 19.7 us -> none  [block_max(): return field.reshape(rows // 2, 2, cols // 2, 2).max(axis=(1, 3))]
    add x38 -> x0, other arithmetic: 10.5 us -> none  [the longest x31 7.11 us: relax_with(): field + OMEGA * active * (source - apply_op(field, weight)) / (4.0 + weight)]
  transfers between devices with their start and end apart: 176 -> 0, of which waited for: 57 -> 0; matrix products, arithmetic and copies ran while one was open for 25% -> 0% of each run, Pallas kernels for 0% -> 0%
where the time goes in v3:
time: 32.6 us; the launch traced here: 32.4 us
  Pallas kernels  31.8 us (98%)
  between operations  0.64 us (2%)
    pallas_call x1, Pallas kernels, body(): pl.pallas_call(functools.partial(kernel, mesh.shape['lon'], mesh.shape['l...  30.8 us
    pallas_call x1, Pallas kernels, body(): pl.pallas_call(store, out_shape=(pltpu.HBM(block, jnp.float32),) * 2, in_...  0.99 us

profile of v3, /device:TPU:0, one launch (start us, length us, event | category | flops | bytes accessed | tf_op | source)
XLA Modules:
  0.0 32.4 jit_solution(4958909102769349466)
XLA Ops:
  0.6 30.8 %shard_map.59 = (f32[128,1024]{1,0:T(8,128)S(1)}, f32[128,1024]{1,0:T(8,128)S(1)}) custom-call(f32[128,1024]{1,0:T(8,128)} %guide.1, f32[128,1024]{1,0:T(8,128)} %screen.1, s32[128,1024]{1,0:T(8,128)} %valid.1, s32[1,8]{1,0:T(1,128)} %tiles.1), custom_call_target="tpu_custom_call" | custom-call | tf_op jit(solution)/shard_map/pallas_call | solution.py:443
  31.4 1.0 %shard_map.60 = (f32[128,1024]{1,0:T(8,128)}, f32[128,1024]{1,0:T(8,128)}) custom-call(f32[128,1024]{1,0:T(8,128)S(1)} %get-tuple-element.4.a, f32[128,1024]{1,0:T(8,128)S(1)} %get-tuple-element.5.b), custom_call_target="tpu_custom_call" | custom-call | tf_op jit(solution)/shard_map/pallas_call | solution.py:464

commit v4 on v3

--- a/solution.py
+++ b/solution.py
@@ -10,6 +10,7 @@
 OMEGA = 0.8
 MESH = pl.DeviceIdType.MESH
 LANES = 128
+CHUNK = 48
 HALF = LANES // 2
 
 P0, P1, P2, P3 = 4, 2, 1, 1
@@ -42,8 +43,9 @@
         x = src(slice(0, rows))
         lane = lanes_of(x)
         mid[t, 0:rows] = gather(x, ((lane & 31) << 2) + (((lane >> 5) + (4 - t)) & 3))
-    for row in range(0, rows, 16):
-        part = slice(row, row + 16)
+    step = min(rows, 16)
+    for row in range(0, rows, step):
+        part = slice(row, row + step)
         tiles = [mid[t, part] for t in range(4)]
         mixed = barrel(tiles, lanes_of(tiles[0]))
         store(0, part, mixed[0])
@@ -65,49 +67,63 @@
         store(gather(x, (((lane + t) & 3) << 5) + (lane >> 2)))
 
 
-def neighbours(src, i, phases, count, lo, hi):
-    t, p = i // phases, i % phases
-    x = src[i, lo:hi]
-    lane = lanes_of(x)
-    if p > 0:
-        left = src[i - 1, lo:hi]
-    else:
-        last = phases - 1
-        left = pltpu.roll(jnp.where(
-            lane == LANES - 1, src[((t - 1) % count) * phases + last, lo:hi], src[t * phases + last, lo:hi]), 1, 1)
-    if p < phases - 1:
-        right = src[i + 1, lo:hi]
-    else:
-        right = pltpu.roll(jnp.where(
-            lane == 0, src[((t + 1) % count) * phases, lo:hi], src[t * phases, lo:hi]), LANES - 1, 1)
-    return x, ((src[i, lo - 1:hi - 1] + src[i, lo + 1:hi + 1]) + left) + right
-
-
-def sweep(src, dst, g, b, phases, count, lo, hi):
-    for i in range(phases * count):
-        x, near = neighbours(src, i, phases, count, lo, hi)
-        dst[i, lo:hi] = (1.0 - OMEGA) * x + b[i, lo:hi] * (g[i, lo:hi] + near)
+def neighbours(src, t, phases, count, lo, hi, wanted):
+    base, last = t * phases, phases - 1
+    row = [src[base + p, lo:hi] for p in range(phases)]
+    lane = lanes_of(row[0])
+    left = right = None
+    if 0 in wanted:
+        left = pltpu.roll(jnp.where(lane == LANES - 1, src[((t - 1) % count) * phases + last, lo:hi], row[last]), 1, 1)
+    if last in wanted:
+        right = pltpu.roll(jnp.where(lane == 0, src[((t + 1) % count) * phases, lo:hi], row[0]), LANES - 1, 1)
+    row = [left] + row + [right]
+    return [(p, row[p + 1], ((src[base + p, lo - 1:hi - 1] + src[base + p, lo + 1:hi + 1]) + row[p]) + row[p + 2])
+            for p in wanted]
+
+
+def everything(phases, count):
+    return {t: tuple(range(phases)) for t in range(count)}
+
+
+def sweep(src, dst, g, b, phases, count, lo, hi, wanted=None):
+    wanted = wanted or everything(phases, count)
+    for start in range(lo, hi, CHUNK):
+        part = slice(start, min(start + CHUNK, hi))
+        for t in wanted:
+            for p, x, near in neighbours(src, t, phases, count, part.start, part.stop, wanted[t]):
+                i = t * phases + p
+                dst[i, part] = (1.0 - OMEGA) * x + b[i, part] * (g[i, part] + near)
 
 
 def first_sweep(dst, g, b, planes, lo, hi):
-    for i in range(planes):
+    for i in planes:
         dst[i, lo:hi] = b[i, lo:hi] * g[i, lo:hi]
 
 
-def residual_of(src, g, e, i, phases, count, lo, hi):
-    x, near = neighbours(src, i, phases, count, lo, hi)
-    ee = e[i, lo:hi]
-    return jnp.where(ee > 0.0, (g[i, lo:hi] + near) - ee * x, 0.0)
+def residual_of(src, g, e, t, phases, count, lo, hi, wanted):
+    found = []
+    for p, x, near in neighbours(src, t, phases, count, lo, hi, wanted):
+        i = t * phases + p
+        ee = e[i, lo:hi]
+        found.append(jnp.where(ee > 0.0, (g[i, lo:hi] + near) - ee * x, 0.0))
+    return found
+
+
+def column_residual(src, g, e, phases, count, lo, hi, tmp):
+    wanted = everything(phases, count)
+    for start in range(lo, hi, CHUNK):
+        part = slice(start, min(start + CHUNK, hi))
+        for t in wanted:
+            r = residual_of(src, g, e, t, phases, count, part.start, part.stop, wanted[t])
+            for k, p in enumerate(wanted[t][::2]):
+                tmp[(t * phases + p) // 2, part] = r[2 * k] + r[2 * k + 1]
 
 
 def rows_op(src, i, lo, rows, op):
     return op(src[i, pl.ds(lo, rows, stride=2)], src[i, pl.ds(lo + 1, rows, stride=2)])
 
 
-def restrict(src, g, e, phases, count, planes, lo, hi, tmp, out, active, tlo, olo, rows):
-    for i in range(planes):
-        tmp[i, lo:hi] = residual_of(src, g, e, 2 * i, phases, count, lo, hi) + residual_of(
-            src, g, e, 2 * i + 1, phases, count, lo, hi)
+def restrict(tmp, planes, tlo, out, active, olo, rows):
     for i in range(planes):
         out[i, olo:olo + rows] = jnp.where(
             active[i, olo:olo + rows] > 0.0, rows_op(tmp, i, tlo, rows, jnp.add), 0.0)
@@ -161,8 +177,8 @@
 
 
 def kernel(lon_count, lat_count, guide, screen, valid, tiles, out, res,
-           gin, win, vin, fin, nat, mid, s0, b0, e0, v0, w0, tmp, vg, bb, e1, u1, wa, b2, e2, gg, v2, u2, r2, b3, g3, v3, u3,
-           xbb, xwa, rvg, in_sem, out_sem, send_sem, recv_sem):
+           gin, win, vin, fin, nat, pack0, land0, mid, s0, b0, e0, v0, w0, tmp, vg, bb, e1, u1, wa, b2, e2, gg, v2, u2, r2, b3, g3, v3, u3,
+           xbb, xwa, rvg, in_sem, send_sem, recv_sem):
     lon = lax.axis_index("lon")
     lat = lax.axis_index("lat")
     v1, g1, b1 = vg.at[0], vg.at[1], bb.at[0]
@@ -232,18 +248,17 @@
             return pl.ds(first + rows - depth - skip, depth), pl.ds(first - depth - skip, depth)
         return (pl.ds(first, rows),) * 2
 
-    first_parts, far_parts = {}, {}
+    near_parts, far_parts, side_parts = {}, {}, {}
     for d, (dy, dx) in enumerate(DIRS):
         if dx == 0:
-            own = pl.ds(0, OWN)
-            for parts, skip in ((first_parts, 0), (far_parts, 8)):
+            for parts, skip in ((near_parts, 0), (far_parts, 8)):
                 a, b = row_spans(dy, H0, N0, 8, skip)
-                parts[d] = nat.at[:, own, a], nat.at[:, own, b]
+                parts[d] = nat.at[:, :, a], nat.at[:, :, b]
         else:
             a, b = row_spans(dy, H0, N0, H0)
-            mine, theirs = (0, OWN) if dx < 0 else (OWN - 2, OWN + 2)
-            first_parts[d] = nat.at[:, pl.ds(mine, 2), a], nat.at[:, pl.ds(theirs, 2), b]
-    first_message, far_message = (0, first_parts), (1, far_parts)
+            side = 0 if dx < 0 else 1
+            side_parts[d] = pack0.at[side, :, a], land0.at[side, :, b]
+    near_message, far_message, side_message = (0, near_parts), (1, far_parts), (0, side_parts)
 
     def coarse_parts(ref, land, phases, first, rows, depth):
         parts = {}
@@ -276,9 +291,17 @@
         active = vin[:, cols].astype(jnp.float32) * fin[0, t].astype(jnp.float32)
         nat[0, t, H0:H0 + N0] = active * gin[:, cols]
         nat[1, t, H0:H0 + N0] = active * OMEGA / (4.0 + win[:, cols])
+    own = slice(H0, H0 + N0)
+    for side, near, far in ((0, 0, 1), (1, OWN - 1, OWN - 2)):
+        for k in range(2):
+            pack0[side, k, own] = nat[k, near, own]
+        source, weight = nat[0, far, own], pltpu.roll(nat[1, far, own], HALF, 1)
+        low = lanes_of(source) < HALF
+        pack0[side, 2, own] = jnp.where(low, source, weight) if side == 0 else jnp.where(low, weight, source)
     interior = jnp.logical_and(lat > 0, lat < lat_count - 1).astype(jnp.int32)
     pl.semaphore_wait(barrier, 5 + 3 * interior)
-    send(first_message)
+    send(side_message)
+    send(near_message)
     send(far_message)
 
     def arrange(t, lo, hi):
@@ -286,8 +309,20 @@
             def store(p, part, x, ref=ref):
                 ref[P0 * t + p, lo + O0 - H0 + part.start:lo + O0 - H0 + part.stop] = x
 
-            split_phases([lambda part, j=j: nat[k, 4 * t + j, lo + part.start:lo + part.stop] for j in range(4)],
-                         mid.at[k], hi - lo, store)
+            def tile(j, part):
+                rows = slice(lo + part.start, lo + part.stop)
+                if t < 2:
+                    return nat[k, 4 * t + j, rows]
+                side = 0 if j < 2 else 1
+                if j in (0, 3):
+                    return land0[side, k, rows]
+                x = land0[side, 2, rows]
+                if k == 1:
+                    x = pltpu.roll(x, HALF, 1)
+                low = lanes_of(x) < HALF
+                return jnp.where(low, x, 0.0) if side == 0 else jnp.where(low, 0.0, x)
+
+            split_phases([functools.partial(tile, j) for j in range(4)], mid.at[k], hi - lo, store)
 
     def columns(t):
         return slice(t * LANES, (t + 1) * LANES)
@@ -322,23 +357,38 @@
     message2 = (3, coarse_parts(wa, xwa, P2, O2, N2, H2))
     send(message2)
 
-    received(first_message)
-    received(far_message)
-    clear((nat.at[0], nat.at[1]), (0, H0), (H0 + N0, 2 * H0 + N0))
-    for t in range(T0):
-        for lo, hi in ((0, 2 * H0 + N0),) if t == T0 - 1 else ((0, H0), (H0 + N0, 2 * H0 + N0)):
+    clear((nat.at[0], nat.at[1], land0.at[0], land0.at[1]), (0, H0), (H0 + N0, 2 * H0 + N0))
+
+    def inverse(t, lo, hi):
+        for i in range(P0 * t, P0 * t + P0):
+            e0[i, lo + 8:hi + 8] = masked_inverse(b0[i, lo + 8:hi + 8])
+
+    received(near_message)
+    for t in range(T0 - 1):
+        for lo, hi in ((8, H0), (H0 + N0, H0 + N0 + 8)):
             arrange(t, lo, hi)
-            for i in range(P0 * t, P0 * t + P0):
-                e0[i, lo + 8:hi + 8] = masked_inverse(b0[i, lo + 8:hi + 8])
+            inverse(t, lo, hi)
+
+    own = range(2 * P0)
+    sides = range(2 * P0, n0)
+    before, after = {0: (1, 2, 3), 1: (0, 1, 2)}, {0: (0,), 1: (3,), 2: (0, 1, 2, 3)}
+    first_sweep(w0, s0, b0, own, *B0)
+    sweep(w0, v0, s0, b0, P0, T0, *B0, before)
+
+    received(side_message)
+    arrange(T0 - 1, 0, 2 * H0 + N0)
+    inverse(T0 - 1, 0, 2 * H0 + N0)
+    first_sweep(w0, s0, b0, sides, *B0)
+    sweep(w0, v0, s0, b0, P0, T0, *B0, after)
+    column_residual(v0, s0, e0, P0, T0, *B0, tmp)
 
     for cycle in range(2):
         rows0 = A0 if cycle == 0 else B0
         g2 = gg.at[cycle]
-        if cycle == 0:
-            first_sweep(w0, s0, b0, n0, *rows0)
-        else:
-            sweep(v0, w0, s0, b0, P0, T0, *rows0)
-        sweep(w0, v0, s0, b0, P0, T0, *rows0)
+        if cycle == 1:
+            sweep(v0, w0, s0, b0, P0, T0, *B0)
+            sweep(w0, v0, s0, b0, P0, T0, *B0)
+            column_residual(v0, s0, e0, P0, T0, *B0, tmp)
 
         if cycle == 0:
             received(message1)
@@ -346,8 +396,8 @@
             merge(xbb, 0, b1, P1, *A1)
             for i in range(n1):
                 e1[i, A1[0]:A1[1]] = masked_inverse(b1[i, A1[0]:A1[1]])
-        restrict(v0, s0, e0, P0, T0, n1, *B0, tmp, g1, b1, A0[0], A1[0], A1[1] - A1[0])
-        first_sweep(u1, g1, b1, n1, *A1)
+        restrict(tmp, n1, A0[0], g1, b1, A1[0], A1[1] - A1[0])
+        first_sweep(u1, g1, b1, range(n1), *A1)
         sweep(u1, v1, g1, b1, P1, T1, *A1)
         if cycle == 0:
             received(message2)
@@ -355,13 +405,21 @@
                   (O2 - H2, O2), (O2 + N2, O2 + N2 + H2))
             for k in range(2):
                 merge(xwa, k, wa.at[k], P2, *A2)
-        restrict(v1, g1, e1, P1, T1, n2, O1, O1 + N1, tmp, g2, a2, O1, O2, N2)
+        column_residual(v1, g1, e1, P1, T1, O1, O1 + N1, tmp)
+        restrict(tmp, n2, O1, g2, a2, O2, N2)
         message_g = (4 + cycle, row_parts(g2, g2, O2, N2, H2))
         message_v = (6 + cycle, row_parts(vg, rvg.at[cycle], O1, N1, H1))
         send(message_g)
         send(message_v)
 
         if cycle == 0:
+            received(far_message)
+            for lo, hi in ((0, 8), (H0 + N0 + 8, 2 * H0 + N0)):
+                for t in range(T0 - 1):
+                    arrange(t, lo, hi)
+                first_sweep(w0, s0, b0, range(n0), lo + 8, hi + 8)
+            for lo, hi in ((A0[0], A0[0] + 16), (A0[1] - 16, A0[1])):
+                sweep(w0, v0, s0, b0, P0, T0, lo, hi)
             lo, hi = A2
             for t in range(n2):
                 diag = 4.0 + w2[t, lo:hi]
@@ -373,14 +431,14 @@
                     4.0 + pack(w2, t, A2[0], hi - lo, jnp.add))
         received(message_g)
         clear((g2,), (O2 - H2, O2), (O2 + N2, O2 + N2 + H2))
-        first_sweep(u2, g2, b2, n2, *A2)
+        first_sweep(u2, g2, b2, range(n2), *A2)
         sweep(u2, v2, g2, b2, P2, T2, *A2)
         for t in range(n2):
-            r2[t, A2[0]:A2[1]] = residual_of(v2, g2, e2, t, P2, T2, *A2)
+            r2[t, A2[0]:A2[1]] = residual_of(v2, g2, e2, t, P2, T2, *A2, (0,))[0]
         lo, hi = A3
         for t in range(n3):
             g3[t, lo:hi] = jnp.where(b3[t, lo:hi] > 0.0, pack(r2, t, A2[0], hi - lo, jnp.add), 0.0)
-        first_sweep(v3, g3, b3, n3, *A3)
+        first_sweep(v3, g3, b3, range(n3), *A3)
         for i in range(7):
             src, dst = (v3, u3) if i % 2 == 0 else (u3, v3)
             sweep(src, dst, g3, b3, P3, T3, *A3)
@@ -403,11 +461,11 @@
         sweep(v0, w0, s0, b0, P0, T0, *rows0)
         sweep(w0, v0, s0, b0, P0, T0, *rows0)
 
-    stores = []
-    for k, (stage, dst) in enumerate(((gin, out), (win, res))):
+    for k, stage in enumerate((out, res)):
         if k == 1:
-            for i in range(2 * P0):
-                w0[i, O0:O0 + N0] = residual_of(v0, s0, e0, i, P0, T0, O0, O0 + N0)
+            for t in range(2):
+                for p, r in enumerate(residual_of(v0, s0, e0, t, P0, T0, O0, O0 + N0, tuple(range(P0)))):
+                    w0[P0 * t + p, O0:O0 + N0] = r
         src = w0 if k == 1 else v0
         for t in range(2):
             def store_tile(j, x):
@@ -415,12 +473,8 @@
 
             join_phases([lambda part, p=p: src[P0 * t + p, part.start + O0:part.stop + O0] for p in range(P0)],
                         mid.at[t], N0, [functools.partial(store_tile, j) for j in range(4)])
-        stores.append(pltpu.make_async_copy(stage, dst, out_sem.at[k]))
-        stores[-1].start()
-    for message in (first_message, far_message, message1, message2):
+    for message in (side_message, near_message, far_message, message1, message2):
         sent(message)
-    for copy in stores:
-        copy.wait()
 
 
 def store(a, b, out, res, sem):
@@ -444,18 +498,18 @@
             functools.partial(kernel, mesh.shape["lon"], mesh.shape["lat"]),
             out_shape=(pltpu.VMEM(block, jnp.float32),) * 2,
             in_specs=[pl.BlockSpec(memory_space=pl.ANY)] * 4,
-            out_specs=(pl.BlockSpec(memory_space=pl.ANY),) * 2,
+            out_specs=(pl.BlockSpec(memory_space=pltpu.VMEM),) * 2,
             scratch_shapes=[
                 pltpu.VMEM(block, jnp.float32), pltpu.VMEM(block, jnp.float32), pltpu.VMEM(block, jnp.int32),
                 pltpu.SMEM((1, OWN), jnp.int32),
-                vmem(2, OWN + 4, N0 + 2 * H0), vmem(2, 4, N0 + 2 * H0), vmem(n0, R0), vmem(n0, R0), vmem(n0, R0), vmem(n0, R0), vmem(n0, R0),
+                vmem(2, OWN, N0 + 2 * H0), vmem(2, 3, N0 + 2 * H0), vmem(2, 3, N0 + 2 * H0), vmem(2, 4, N0 + 2 * H0), vmem(n0, R0), vmem(n0, R0), vmem(n0, R0), vmem(n0, R0), vmem(n0, R0),
                 vmem(n1, R0),
                 vmem(2, n1, R1), vmem(1, n1, R1), vmem(n1, R1), vmem(n1, R1),
                 vmem(2, n2, R2), vmem(n2, R2), vmem(n2, R2), vmem(2, n2, R2), vmem(n2, R2), vmem(n2, R2), vmem(n2, R2),
                 vmem(n3, R3), vmem(n3, R3), vmem(n3, R3), vmem(n3, R3),
                 vmem(2, 1, P1, R1), vmem(2, 2, P2, R2), vmem(2, 2, n1, R1),
-                pltpu.SemaphoreType.DMA((4,)), pltpu.SemaphoreType.DMA((2,)),
-                pltpu.SemaphoreType.DMA((8, 8)), pltpu.SemaphoreType.DMA((8, 8)),
+                pltpu.SemaphoreType.DMA((4,)), pltpu.SemaphoreType.DMA((8, 8)),
+                pltpu.SemaphoreType.DMA((8, 8)),
             ],
             compiler_params=pltpu.CompilerParams(
                 collective_id=0, has_side_effects=True, vmem_limit_bytes=48 * 1024 * 1024),

time: 32.6 us -> 30.4 us (0.933)
  Pallas kernels: 31.8 us -> 29.7 us
    pallas_call x1, Pallas kernels: 30.8 us -> 28.7 us  [body(): pl.pallas_call(functools.partial(kernel, mesh.shape['lon'], mesh.shape['l...]
where the time goes in v4:
time: 30.4 us; the launch traced here: 30.3 us
  Pallas kernels  29.7 us (98%)
  between operations  0.64 us (2%)
    pallas_call x1, Pallas kernels, body(): pl.pallas_call(functools.partial(kernel, mesh.shape['lon'], mesh.shape['l...  28.7 us
    pallas_call x1, Pallas kernels, body(): pl.pallas_call(store, out_shape=(pltpu.HBM(block, jnp.float32),) * 2, in_...  0.99 us

profile of v4, /device:TPU:0, one launch (start us, length us, event | category | flops | bytes accessed | tf_op | source)
XLA Modules:
  0.0 30.3 jit_solution(11627943415946471100)
XLA Ops:
  0.6 28.7 %shard_map.59 = (f32[128,1024]{1,0:T(8,128)S(1)}, f32[128,1024]{1,0:T(8,128)S(1)}) custom-call(f32[128,1024]{1,0:T(8,128)} %guide.1, f32[128,1024]{1,0:T(8,128)} %screen.1, s32[128,1024]{1,0:T(8,128)} %valid.1, s32[1,8]{1,0:T(1,128)} %tiles.1), custom_call_target="tpu_custom_call" | custom-call | tf_op jit(solution)/shard_map/pallas_call | solution.py:497
  29.3 1.0 %shard_map.60 = (f32[128,1024]{1,0:T(8,128)}, f32[128,1024]{1,0:T(8,128)}) custom-call(f32[128,1024]{1,0:T(8,128)S(1)} %get-tuple-element.4.a, f32[128,1024]{1,0:T(8,128)S(1)} %get-tuple-element.5.b), custom_call_target="tpu_custom_call" | custom-call | tf_op jit(solution)/shard_map/pallas_call | solution.py:518

commit v5 on v4

--- a/solution.py
+++ b/solution.py
@@ -10,7 +10,7 @@
 OMEGA = 0.8
 MESH = pl.DeviceIdType.MESH
 LANES = 128
-CHUNK = 48
+CHUNK = 24
 HALF = LANES // 2
 
 P0, P1, P2, P3 = 4, 2, 1, 1
@@ -18,7 +18,7 @@
 O0, O1, O2, O3 = 24, 16, 32, 20
 N0, N1, N2, N3 = 128, 64, 32, 16
 R0, R1, R2, R3 = 176, 96, 96, 56
-A0, B0, A1, A2, A3 = (8, 168), (16, 160), (8, 88), (8, 88), (8, 48)
+A0, B0, A1, A2, B2, A3 = (8, 168), (16, 160), (8, 88), (8, 88), (24, 72), (8, 48)
 H0, H1, H2 = 16, 8, 24
 OWN = 8
 DIRS = ((-1, 0), (1, 0), (0, -1), (0, 1), (-1, -1), (-1, 1), (1, -1), (1, 1))
@@ -38,15 +38,16 @@
     return [jnp.where(high, half[(i + 2) % 4], half[i]) for i in range(4)]
 
 
-def split_phases(sources, mid, rows, store):
-    for t, src in enumerate(sources):
-        x = src(slice(0, rows))
-        lane = lanes_of(x)
-        mid[t, 0:rows] = gather(x, ((lane & 31) << 2) + (((lane >> 5) + (4 - t)) & 3))
+def group_phases(x, t):
+    lane = lanes_of(x)
+    return gather(x, ((lane & 31) << 2) + (((lane >> 5) + (4 - t)) & 3))
+
+
+def split_phases(sources, rows, store):
     step = min(rows, 16)
     for row in range(0, rows, step):
         part = slice(row, row + step)
-        tiles = [mid[t, part] for t in range(4)]
+        tiles = [src(part) for src in sources]
         mixed = barrel(tiles, lanes_of(tiles[0]))
         store(0, part, mixed[0])
         for p in range(1, 4):
@@ -67,7 +68,7 @@
         store(gather(x, (((lane + t) & 3) << 5) + (lane >> 2)))
 
 
-def neighbours(src, t, phases, count, lo, hi, wanted):
+def neighbours(src, g, t, phases, count, lo, hi, wanted):
     base, last = t * phases, phases - 1
     row = [src[base + p, lo:hi] for p in range(phases)]
     lane = lanes_of(row[0])
@@ -77,8 +78,8 @@
     if last in wanted:
         right = pltpu.roll(jnp.where(lane == 0, src[((t + 1) % count) * phases, lo:hi], row[0]), LANES - 1, 1)
     row = [left] + row + [right]
-    return [(p, row[p + 1], ((src[base + p, lo - 1:hi - 1] + src[base + p, lo + 1:hi + 1]) + row[p]) + row[p + 2])
-            for p in wanted]
+    return [(p, row[p + 1], (g[base + p, lo:hi] + (src[base + p, lo - 1:hi - 1] + src[base + p, lo + 1:hi + 1])) + (
+        row[p] + row[p + 2])) for p in wanted]
 
 
 def everything(phases, count):
@@ -90,9 +91,9 @@
     for start in range(lo, hi, CHUNK):
         part = slice(start, min(start + CHUNK, hi))
         for t in wanted:
-            for p, x, near in neighbours(src, t, phases, count, part.start, part.stop, wanted[t]):
+            for p, x, near in neighbours(src, g, t, phases, count, part.start, part.stop, wanted[t]):
                 i = t * phases + p
-                dst[i, part] = (1.0 - OMEGA) * x + b[i, part] * (g[i, part] + near)
+                dst[i, part] = (1.0 - OMEGA) * x + b[i, part] * near
 
 
 def first_sweep(dst, g, b, planes, lo, hi):
@@ -102,10 +103,10 @@
 
 def residual_of(src, g, e, t, phases, count, lo, hi, wanted):
     found = []
-    for p, x, near in neighbours(src, t, phases, count, lo, hi, wanted):
+    for p, x, near in neighbours(src, g, t, phases, count, lo, hi, wanted):
         i = t * phases + p
         ee = e[i, lo:hi]
-        found.append(jnp.where(ee > 0.0, (g[i, lo:hi] + near) - ee * x, 0.0))
+        found.append(jnp.where(ee > 0.0, near - ee * x, 0.0))
     return found
 
 
@@ -199,14 +200,29 @@
             pl.when(condition)(fn)
 
     barrier = pltpu.get_barrier_semaphore()
-    for d in range(8):
-        guarded(exists(DIRS[d][0]), lambda d=d: pl.semaphore_signal(
-            barrier, inc=1, device_id=peer(d), device_id_type=MESH))
-
-    loads = [pltpu.make_async_copy(src, dst, in_sem.at[i]) for i, (src, dst) in enumerate((
-        (valid, vin), (screen, win), (guide, gin), (tiles, fin)))]
-    for copy in loads:
-        copy.start()
+    def by_row(directions, fn, sign=1):
+        for dy in (-1, 1, 0):
+            chosen = [d for d in directions if DIRS[d][0] == dy]
+
+            def run(chosen=chosen):
+                for d in chosen:
+                    fn(d)
+
+            if chosen:
+                guarded(exists(sign * dy), run)
+
+    by_row(range(8), lambda d: pl.semaphore_signal(barrier, inc=1, device_id=peer(d), device_id_type=MESH))
+
+    outer, inner = (0, 1, OWN - 2, OWN - 1), tuple(range(2, OWN - 2))
+    flag_copy = pltpu.make_async_copy(tiles, fin, in_sem.at[3, 0])
+    loads = [[pltpu.make_async_copy(src.at[:, cols], dst.at[:, cols], in_sem.at[i, k])
+              for i, (src, dst) in enumerate(((valid, vin), (screen, win), (guide, gin)))]
+             for k, cols in enumerate((pl.ds(0, 2 * LANES), pl.ds((OWN - 2) * LANES, 2 * LANES),
+                                       pl.ds(2 * LANES, (OWN - 4) * LANES)))]
+    flag_copy.start()
+    for part in loads:
+        for copy in part:
+            copy.start()
 
     for ref, lo, hi in ((v0, *A0), (w0, *A0), (v1, *A1), (u1, *A1), (v2, *A2), (u2, *A2), (v3, *A3), (u3, *A3)):
         zero = jnp.zeros((ref.shape[0], 8, LANES), jnp.float32)
@@ -221,16 +237,13 @@
             device_id=peer(d), device_id_type=MESH)
 
     def send(message):
-        for d in message[1]:
-            guarded(exists(DIRS[d][0]), lambda d=d: copy_of(message, d).start())
+        by_row(message[1], lambda d: copy_of(message, d).start())
 
     def sent(message):
-        for d in message[1]:
-            guarded(exists(DIRS[d][0]), lambda d=d: copy_of(message, d).wait_send())
+        by_row(message[1], lambda d: copy_of(message, d).wait_send())
 
     def received(message):
-        for d in message[1]:
-            guarded(exists(-DIRS[d][0]), lambda d=d: copy_of(message, d).wait_recv())
+        by_row(message[1], lambda d: copy_of(message, d).wait_recv(), -1)
 
     def clear(refs, above, below):
         for edge, rows in ((lat == 0, above), (lat == lat_count - 1, below)):
@@ -284,61 +297,77 @@
             left = land[0, k, p, lo:hi]
             ref[2 * phases + p, lo:hi] = jnp.where(lanes_of(left) < HALF, land[1, k, p, lo:hi], left)
 
-    for copy in loads:
-        copy.wait()
-    for t in range(OWN):
+    def prepare(t):
         cols = slice(t * LANES, (t + 1) * LANES)
         active = vin[:, cols].astype(jnp.float32) * fin[0, t].astype(jnp.float32)
         nat[0, t, H0:H0 + N0] = active * gin[:, cols]
         nat[1, t, H0:H0 + N0] = active * OMEGA / (4.0 + win[:, cols])
+
+    flag_copy.wait()
+    for copy in loads[0] + loads[1]:
+        copy.wait()
+    for t in outer:
+        prepare(t)
     own = slice(H0, H0 + N0)
     for side, near, far in ((0, 0, 1), (1, OWN - 1, OWN - 2)):
         for k in range(2):
-            pack0[side, k, own] = nat[k, near, own]
-        source, weight = nat[0, far, own], pltpu.roll(nat[1, far, own], HALF, 1)
-        low = lanes_of(source) < HALF
-        pack0[side, 2, own] = jnp.where(low, source, weight) if side == 0 else jnp.where(low, weight, source)
+            pack0[side, k, own] = group_phases(nat[k, near, own], near % 4)
+        source, weight = group_phases(nat[0, far, own], far % 4), group_phases(nat[1, far, own], far % 4)
+        low = (lanes_of(source) & 16) == 0
+        if side == 0:
+            pack0[side, 2, own] = jnp.where(low, source, pltpu.roll(weight, 16, 1))
+        else:
+            pack0[side, 2, own] = jnp.where(low, pltpu.roll(weight, LANES - 16, 1), source)
     interior = jnp.logical_and(lat > 0, lat < lat_count - 1).astype(jnp.int32)
     pl.semaphore_wait(barrier, 5 + 3 * interior)
     send(side_message)
+    for copy in loads[2]:
+        copy.wait()
+    for t in inner:
+        prepare(t)
     send(near_message)
     send(far_message)
 
-    def arrange(t, lo, hi):
-        for k, ref in enumerate((s0, b0)):
+    def arrange(t, lo, hi, arrays=(0, 1)):
+        for k in arrays:
+            ref = (s0, b0)[k]
+
             def store(p, part, x, ref=ref):
                 ref[P0 * t + p, lo + O0 - H0 + part.start:lo + O0 - H0 + part.stop] = x
 
             def tile(j, part):
+                if t < 2:
+                    return mid[k, j, part]
                 rows = slice(lo + part.start, lo + part.stop)
-                if t < 2:
-                    return nat[k, 4 * t + j, rows]
                 side = 0 if j < 2 else 1
                 if j in (0, 3):
                     return land0[side, k, rows]
                 x = land0[side, 2, rows]
                 if k == 1:
-                    x = pltpu.roll(x, HALF, 1)
-                low = lanes_of(x) < HALF
+                    x = pltpu.roll(x, LANES - 16 if side == 0 else 16, 1)
+                low = (lanes_of(x) & 16) == 0
                 return jnp.where(low, x, 0.0) if side == 0 else jnp.where(low, 0.0, x)
 
-            split_phases([functools.partial(tile, j) for j in range(4)], mid.at[k], hi - lo, store)
+            if t < 2:
+                for j in range(4):
+                    mid[k, j, 0:hi - lo] = group_phases(nat[k, 4 * t + j, lo:hi], j)
+            split_phases([functools.partial(tile, j) for j in range(4)], hi - lo, store)
 
     def columns(t):
         return slice(t * LANES, (t + 1) * LANES)
 
     for t in range(2):
-        arrange(t, H0, H0 + N0)
+        arrange(t, H0, H0 + N0, (1,))
 
         def store_weight(p, part, x):
             w0[P0 * t + p, part.start + O0:part.stop + O0] = x
 
-        split_phases([lambda part, j=j: win[part, columns(4 * t + j)] for j in range(4)], mid.at[0], N0, store_weight)
+        for j in range(4):
+            mid[0, j, 0:N0] = group_phases(win[:, columns(4 * t + j)], j)
+        split_phases([lambda part, j=j: mid[0, j, part] for j in range(4)], N0, store_weight)
     own = slice(O0, O0 + N0)
     for i in range(2 * P0):
-        on = b0[i, own] > 0.0
-        e0[i, own] = jnp.where(on, 4.0 + w0[i, own], 0.0)
-        v0[i, own] = jnp.where(on, 1.0, 0.0)
+        v0[i, own] = jnp.where(b0[i, own] > 0.0, 1.0, 0.0)
 
     own = slice(O1, O1 + N1)
     for i in range(2 * P1):
@@ -357,6 +386,12 @@
     message2 = (3, coarse_parts(wa, xwa, P2, O2, N2, H2))
     send(message2)
 
+    own = slice(O0, O0 + N0)
+    for t in range(2):
+        arrange(t, H0, H0 + N0, (0,))
+    for i in range(2 * P0):
+        e0[i, own] = jnp.where(b0[i, own] > 0.0, 4.0 + w0[i, own], 0.0)
+
     clear((nat.at[0], nat.at[1], land0.at[0], land0.at[1]), (0, H0), (H0 + N0, 2 * H0 + N0))
 
     def inverse(t, lo, hi):
@@ -399,14 +434,10 @@
         restrict(tmp, n1, A0[0], g1, b1, A1[0], A1[1] - A1[0])
         first_sweep(u1, g1, b1, range(n1), *A1)
         sweep(u1, v1, g1, b1, P1, T1, *A1)
-        if cycle == 0:
-            received(message2)
-            clear((w2, a2, xwa.at[0, 0], xwa.at[0, 1], xwa.at[1, 0], xwa.at[1, 1]),
-                  (O2 - H2, O2), (O2 + N2, O2 + N2 + H2))
-            for k in range(2):
-                merge(xwa, k, wa.at[k], P2, *A2)
         column_residual(v1, g1, e1, P1, T1, O1, O1 + N1, tmp)
-        restrict(tmp, n2, O1, g2, a2, O2, N2)
+        for t in range(n2):
+            on = coarsen(b1, t, O1, N2, jnp.maximum) > 0.0
+            g2[t, O2:O2 + N2] = jnp.where(on, rows_op(tmp, t, O1, N2, jnp.add), 0.0)
         message_g = (4 + cycle, row_parts(g2, g2, O2, N2, H2))
         message_v = (6 + cycle, row_parts(vg, rvg.at[cycle], O1, N1, H1))
         send(message_g)
@@ -420,6 +451,11 @@
                 first_sweep(w0, s0, b0, range(n0), lo + 8, hi + 8)
             for lo, hi in ((A0[0], A0[0] + 16), (A0[1] - 16, A0[1])):
                 sweep(w0, v0, s0, b0, P0, T0, lo, hi)
+            received(message2)
+            clear((w2, a2, xwa.at[0, 0], xwa.at[0, 1], xwa.at[1, 0], xwa.at[1, 1]),
+                  (O2 - H2, O2), (O2 + N2, O2 + N2 + H2))
+            for k in range(2):
+                merge(xwa, k, wa.at[k], P2, *A2)
             lo, hi = A2
             for t in range(n2):
                 diag = 4.0 + w2[t, lo:hi]
@@ -442,9 +478,9 @@
         for i in range(7):
             src, dst = (v3, u3) if i % 2 == 0 else (u3, v3)
             sweep(src, dst, g3, b3, P3, T3, *A3)
-        unpack(u3, v2, b2, A3[0], hi - lo, A2[0], tmp)
-        sweep(v2, u2, g2, b2, P2, T2, *A2)
-        sweep(u2, v2, g2, b2, P2, T2, *A2)
+        unpack(u3, v2, b2, A3[0] + (B2[0] - A2[0]) // 2, (B2[1] - B2[0]) // 2, B2[0], tmp)
+        sweep(v2, u2, g2, b2, P2, T2, *B2)
+        sweep(u2, v2, g2, b2, P2, T2, *B2)
 
         sent(message_g)
         sent(message_v)
@@ -461,26 +497,28 @@
         sweep(v0, w0, s0, b0, P0, T0, *rows0)
         sweep(w0, v0, s0, b0, P0, T0, *rows0)
 
-    for k, stage in enumerate((out, res)):
-        if k == 1:
-            for t in range(2):
-                for p, r in enumerate(residual_of(v0, s0, e0, t, P0, T0, O0, O0 + N0, tuple(range(P0)))):
-                    w0[P0 * t + p, O0:O0 + N0] = r
-        src = w0 if k == 1 else v0
+    own = slice(O0, O0 + N0)
+    for t in range(2):
+        for p, r in enumerate(residual_of(v0, s0, e0, t, P0, T0, own.start, own.stop, tuple(range(P0)))):
+            i = P0 * t + p
+            out[i] = v0[i, own]
+            res[i] = r
+    for message in (side_message, near_message, far_message, message1, message2):
+        sent(message)
+
+
+def store(a, b, out, res, stage, mid, sem):
+    copies = []
+    for k, (src, dst) in enumerate(((a, out), (b, res))):
         for t in range(2):
             def store_tile(j, x):
-                stage[:, columns(4 * t + j)] = x
-
-            join_phases([lambda part, p=p: src[P0 * t + p, part.start + O0:part.stop + O0] for p in range(P0)],
-                        mid.at[t], N0, [functools.partial(store_tile, j) for j in range(4)])
-    for message in (side_message, near_message, far_message, message1, message2):
-        sent(message)
-
-
-def store(a, b, out, res, sem):
-    copies = [pltpu.make_async_copy(x, y, sem.at[i]) for i, (x, y) in enumerate(((a, out), (b, res)))]
-    for copy in copies:
-        copy.start()
+                stage[k, :, (4 * t + j) * LANES:(4 * t + j + 1) * LANES] = x
+
+            join_phases([lambda part, p=p: src[P0 * t + p, part] for p in range(P0)], mid, N0,
+                        [functools.partial(store_tile, j) for j in range(4)])
+            half = pl.ds(4 * t * LANES, 4 * LANES)
+            copies.append(pltpu.make_async_copy(stage.at[k, :, half], dst.at[:, half], sem.at[k, t]))
+            copies[-1].start()
     for copy in copies:
         copy.wait()
 
@@ -496,7 +534,7 @@
             pltpu.with_memory_space_constraint(x, pltpu.HBM) for x in (guide, screen, valid, tiles)]
         pair = pl.pallas_call(
             functools.partial(kernel, mesh.shape["lon"], mesh.shape["lat"]),
-            out_shape=(pltpu.VMEM(block, jnp.float32),) * 2,
+            out_shape=(pltpu.VMEM((2 * P0, N0, LANES), jnp.float32),) * 2,
             in_specs=[pl.BlockSpec(memory_space=pl.ANY)] * 4,
             out_specs=(pl.BlockSpec(memory_space=pltpu.VMEM),) * 2,
             scratch_shapes=[
@@ -508,7 +546,7 @@
                 vmem(2, n2, R2), vmem(n2, R2), vmem(n2, R2), vmem(2, n2, R2), vmem(n2, R2), vmem(n2, R2), vmem(n2, R2),
                 vmem(n3, R3), vmem(n3, R3), vmem(n3, R3), vmem(n3, R3),
                 vmem(2, 1, P1, R1), vmem(2, 2, P2, R2), vmem(2, 2, n1, R1),
-                pltpu.SemaphoreType.DMA((4,)), pltpu.SemaphoreType.DMA((8, 8)),
+                pltpu.SemaphoreType.DMA((4, 3)), pltpu.SemaphoreType.DMA((8, 8)),
                 pltpu.SemaphoreType.DMA((8, 8)),
             ],
             compiler_params=pltpu.CompilerParams(
@@ -518,9 +556,9 @@
         return pl.pallas_call(
             store,
             out_shape=(pltpu.HBM(block, jnp.float32),) * 2,
-            in_specs=[pl.BlockSpec(memory_space=pl.ANY)] * 2,
+            in_specs=[pl.BlockSpec(memory_space=pltpu.VMEM)] * 2,
             out_specs=(pl.BlockSpec(memory_space=pltpu.HBM),) * 2,
-            scratch_shapes=[pltpu.SemaphoreType.DMA((2,))],
+            scratch_shapes=[pltpu.VMEM((2,) + block, jnp.float32), vmem(4, N0), pltpu.SemaphoreType.DMA((2, 2))],
         )(*pair)
 
     spec = P("lat", "lon")

time: 30.4 us -> 29.9 us (0.984)
  Pallas kernels: 29.7 us -> 29.1 us
    pallas_call x1, Pallas kernels: 28.7 us -> 27.3 us  [body(): pl.pallas_call(functools.partial(kernel, mesh.shape['lon'], mesh.shape['l...]
    pallas_call x1, Pallas kernels: 0.99 us -> 1.84 us  [body(): pl.pallas_call(store, out_shape=(pltpu.HBM(block, jnp.float32),) * 2, in_...]
where the time goes in v5:
time: 29.9 us; the launch traced here: 29.8 us
  Pallas kernels  29.1 us (97%)
  between operations  0.64 us (2%)
    pallas_call x1, Pallas kernels, body(): pl.pallas_call(functools.partial(kernel, mesh.shape['lon'], mesh.shape['l...  27.3 us
    pallas_call x1, Pallas kernels, body(): pl.pallas_call(store, out_shape=(pltpu.HBM(block, jnp.float32),) * 2, in_...  1.84 us

profile of v5, /device:TPU:0, one launch (start us, length us, event | category | flops | bytes accessed | tf_op | source)
XLA Modules:
  0.0 29.8 jit_solution(8144818989551836736)
XLA Ops:
  0.6 27.3 %shard_map.59 = (f32[8,128,128]{2,1,0:T(8,128)S(1)}, f32[8,128,128]{2,1,0:T(8,128)S(1)}) custom-call(f32[128,1024]{1,0:T(8,128)} %guide.1, f32[128,1024]{1,0:T(8,128)} %screen.1, s32[128,1024]{1,0:T(8,128)} %valid.1, s32[1,8]{1,0:T(1,128)} %tiles.1), custom_call_target="tpu_custom_call" | custom-call | tf_op jit(solution)/shard_map/pallas_call | solution.py:535
  27.9 1.8 %shard_map.60 = (f32[128,1024]{1,0:T(8,128)}, f32[128,1024]{1,0:T(8,128)}) custom-call(f32[8,128,128]{2,1,0:T(8,128)S(1)} %get-tuple-element.4.a, f32[8,128,128]{2,1,0:T(8,128)S(1)} %get-tuple-element.5.b), custom_call_target="tpu_custom_call" | custom-call | tf_op jit(solution)/shard_map/pallas_call | solution.py:556

commit v6 on v5

--- a/solution.py
+++ b/solution.py
@@ -261,7 +261,7 @@
             return pl.ds(first + rows - depth - skip, depth), pl.ds(first - depth - skip, depth)
         return (pl.ds(first, rows),) * 2
 
-    near_parts, far_parts, side_parts = {}, {}, {}
+    near_parts, far_parts, side_parts, late_parts = {}, {}, {}, {}
     for d, (dy, dx) in enumerate(DIRS):
         if dx == 0:
             for parts, skip in ((near_parts, 0), (far_parts, 8)):
@@ -270,8 +270,13 @@
         else:
             a, b = row_spans(dy, H0, N0, H0)
             side = 0 if dx < 0 else 1
+            if dy == 0:
+                a, late = (pl.ds(H0 + k * (N0 // 2), N0 // 2) for k in range(2))
+                b = a
+                late_parts[d] = pack0.at[side, :, late], land0.at[side, :, late]
             side_parts[d] = pack0.at[side, :, a], land0.at[side, :, b]
-    near_message, far_message, side_message = (0, near_parts), (1, far_parts), (0, side_parts)
+    near_message, far_message = (0, near_parts), (1, far_parts)
+    side_message, late_message = (0, side_parts), (8, late_parts)
 
     def coarse_parts(ref, land, phases, first, rows, depth):
         parts = {}
@@ -321,6 +326,7 @@
     interior = jnp.logical_and(lat > 0, lat < lat_count - 1).astype(jnp.int32)
     pl.semaphore_wait(barrier, 5 + 3 * interior)
     send(side_message)
+    send(late_message)
     for copy in loads[2]:
         copy.wait()
     for t in inner:
@@ -375,6 +381,7 @@
         weight = coarsen(w0, i, O0, N1, jnp.add)
         diag = 4.0 + weight
         b1[i, own] = active * OMEGA / diag
+        e1[i, own] = active * diag
         v1[i, own] = active
         u1[i, own] = weight
     message1 = (2, coarse_parts(bb, xbb, P1, O1, N1, H1))
@@ -410,9 +417,13 @@
     first_sweep(w0, s0, b0, own, *B0)
     sweep(w0, v0, s0, b0, P0, T0, *B0, before)
 
+    middle, end = H0 + N0 // 2, 2 * H0 + N0
     received(side_message)
-    arrange(T0 - 1, 0, 2 * H0 + N0)
-    inverse(T0 - 1, 0, 2 * H0 + N0)
+    arrange(T0 - 1, 0, middle)
+    inverse(T0 - 1, 0, middle)
+    received(late_message)
+    arrange(T0 - 1, middle, end)
+    inverse(T0 - 1, middle, end)
     first_sweep(w0, s0, b0, sides, *B0)
     sweep(w0, v0, s0, b0, P0, T0, *B0, after)
     column_residual(v0, s0, e0, P0, T0, *B0, tmp)
@@ -429,8 +440,8 @@
             received(message1)
             clear((bb.at[0], xbb.at[0, 0], xbb.at[1, 0]), (O1 - H1, O1), (O1 + N1, O1 + N1 + H1))
             merge(xbb, 0, b1, P1, *A1)
-            for i in range(n1):
-                e1[i, A1[0]:A1[1]] = masked_inverse(b1[i, A1[0]:A1[1]])
+            for i in range(2 * P1, n1):
+                e1[i, O1:O1 + N1] = masked_inverse(b1[i, O1:O1 + N1])
         restrict(tmp, n1, A0[0], g1, b1, A1[0], A1[1] - A1[0])
         first_sweep(u1, g1, b1, range(n1), *A1)
         sweep(u1, v1, g1, b1, P1, T1, *A1)
@@ -503,7 +514,7 @@
             i = P0 * t + p
             out[i] = v0[i, own]
             res[i] = r
-    for message in (side_message, near_message, far_message, message1, message2):
+    for message in (side_message, late_message, near_message, far_message, message1, message2):
         sent(message)
 
 
@@ -546,8 +557,8 @@
                 vmem(2, n2, R2), vmem(n2, R2), vmem(n2, R2), vmem(2, n2, R2), vmem(n2, R2), vmem(n2, R2), vmem(n2, R2),
                 vmem(n3, R3), vmem(n3, R3), vmem(n3, R3), vmem(n3, R3),
                 vmem(2, 1, P1, R1), vmem(2, 2, P2, R2), vmem(2, 2, n1, R1),
-                pltpu.SemaphoreType.DMA((4, 3)), pltpu.SemaphoreType.DMA((8, 8)),
-                pltpu.SemaphoreType.DMA((8, 8)),
+                pltpu.SemaphoreType.DMA((4, 3)), pltpu.SemaphoreType.DMA((9, 8)),
+                pltpu.SemaphoreType.DMA((9, 8)),
             ],
             compiler_params=pltpu.CompilerParams(
                 collective_id=0, has_side_effects=True, vmem_limit_bytes=48 * 1024 * 1024),

time: 29.9 us -> 29.6 us (0.990)
  Pallas kernels: 29.1 us -> 28.8 us
    pallas_call x1, Pallas kernels: 27.3 us -> 27 us  [body(): pl.pallas_call(functools.partial(kernel, mesh.shape['lon'], mesh.shape['l...]
where the time goes in v6:
time: 29.6 us; the launch traced here: 29.4 us
  Pallas kernels  28.8 us (97%)
  between operations  0.64 us (2%)
    pallas_call x1, Pallas kernels, body(): pl.pallas_call(functools.partial(kernel, mesh.shape['lon'], mesh.shape['l...  27 us
    pallas_call x1, Pallas kernels, body(): pl.pallas_call(store, out_shape=(pltpu.HBM(block, jnp.float32),) * 2, in_...  1.84 us

profile of v6, /device:TPU:0, one launch (start us, length us, event | category | flops | bytes accessed | tf_op | source)
XLA Modules:
  0.0 29.4 jit_solution(8748973673848464310)
XLA Ops:
  0.6 27.0 %shard_map.59 = (f32[8,128,128]{2,1,0:T(8,128)S(1)}, f32[8,128,128]{2,1,0:T(8,128)S(1)}) custom-call(f32[128,1024]{1,0:T(8,128)} %guide.1, f32[128,1024]{1,0:T(8,128)} %screen.1, s32[128,1024]{1,0:T(8,128)} %valid.1, s32[1,8]{1,0:T(1,128)} %tiles.1), custom_call_target="tpu_custom_call" | custom-call | tf_op jit(solution)/shard_map/pallas_call | solution.py:546
  27.6 1.8 %shard_map.60 = (f32[128,1024]{1,0:T(8,128)}, f32[128,1024]{1,0:T(8,128)}) custom-call(f32[8,128,128]{2,1,0:T(8,128)S(1)} %get-tuple-element.4.a, f32[8,128,128]{2,1,0:T(8,128)S(1)} %get-tuple-element.5.b), custom_call_target="tpu_custom_call" | custom-call | tf_op jit(solution)/shard_map/pallas_call | solution.py:567

commit v7 on v6

--- a/solution.py
+++ b/solution.py
@@ -421,12 +421,17 @@
     received(side_message)
     arrange(T0 - 1, 0, middle)
     inverse(T0 - 1, 0, middle)
+    lo, hi = B0
+    ready = middle + 8
+    first_sweep(w0, s0, b0, sides, lo, ready)
+    sweep(w0, v0, s0, b0, P0, T0, lo, ready - 8, after)
+    column_residual(v0, s0, e0, P0, T0, lo, ready - 16, tmp)
     received(late_message)
     arrange(T0 - 1, middle, end)
     inverse(T0 - 1, middle, end)
-    first_sweep(w0, s0, b0, sides, *B0)
-    sweep(w0, v0, s0, b0, P0, T0, *B0, after)
-    column_residual(v0, s0, e0, P0, T0, *B0, tmp)
+    first_sweep(w0, s0, b0, sides, ready, hi)
+    sweep(w0, v0, s0, b0, P0, T0, ready - 8, hi, after)
+    column_residual(v0, s0, e0, P0, T0, ready - 16, hi, tmp)
 
     for cycle in range(2):
         rows0 = A0 if cycle == 0 else B0

time: 29.6 us -> 29.6 us (level)
  no operation moved by 1% of the time
where the time goes in v7:
time: 29.6 us; the launch traced here: 29.5 us
  Pallas kernels  28.8 us (97%)
  between operations  0.64 us (2%)
    pallas_call x1, Pallas kernels, body(): pl.pallas_call(functools.partial(kernel, mesh.shape['lon'], mesh.shape['l...  27 us
    pallas_call x1, Pallas kernels, body(): pl.pallas_call(store, out_shape=(pltpu.HBM(block, jnp.float32),) * 2, in_...  1.84 us

profile of v7, /device:TPU:0, one launch (start us, length us, event | category | flops | bytes accessed | tf_op | source)
XLA Modules:
  0.0 29.5 jit_solution(18078463766597968577)
XLA Ops:
  0.6 27.0 %shard_map.59 = (f32[8,128,128]{2,1,0:T(8,128)S(1)}, f32[8,128,128]{2,1,0:T(8,128)S(1)}) custom-call(f32[128,1024]{1,0:T(8,128)} %guide.1, f32[128,1024]{1,0:T(8,128)} %screen.1, s32[128,1024]{1,0:T(8,128)} %valid.1, s32[1,8]{1,0:T(1,128)} %tiles.1), custom_call_target="tpu_custom_call" | custom-call | tf_op jit(solution)/shard_map/pallas_call | solution.py:551
  27.6 1.8 %shard_map.60 = (f32[128,1024]{1,0:T(8,128)}, f32[128,1024]{1,0:T(8,128)}) custom-call(f32[8,128,128]{2,1,0:T(8,128)S(1)} %get-tuple-element.4.a, f32[8,128,128]{2,1,0:T(8,128)S(1)} %get-tuple-element.5.b), custom_call_target="tpu_custom_call" | custom-call | tf_op jit(solution)/shard_map/pallas_call | solution.py:572
